TPU v7x, 128 devices: a whole 4x4x4 slice. The times are simulated.
128 devices in a mesh: dp: 4 (over y_hi, core), context: 32 (over z, x, y_lo).
Axes of the slice: x: 4, y: 4 (y_hi: 2, y_lo: 2; y = y_hi * 2 + y_lo), z: 4, core: 2. Of those that a mesh axis runs over, the one named last changes fastest.
Arguments:
- tokens: bfloat16 [4096, 8192], P('context', 'dp'), may hold values from -6 to 6
- in_weight: bfloat16 [8192, 2, 2048], P(None, None, 'dp'), may hold values from -0.0625 to 0.0625
- short_taps: float32 [2, 3, 2048], P(None, None, 'dp'), may hold values from -1 to 1
- filters: float32 [2048, 4096], P(('dp', 'context')), may hold values from -1 to 1, as said below
- cotangent: bfloat16 [2048, 4096], P('dp', 'context'), may hold values from -1.5 to 1.5
Outputs:
- gated_out: bfloat16 [2048, 4096], P('dp', 'context')
- token_grad: bfloat16 [4096, 8192], P('context', 'dp')
- weight_grad: bfloat16 [8192, 2, 2048], P('context', None, 'dp')
- filter_grad: float32 [2048, 4096], P(('dp', 'context'))
Inputs may be any that keep to these rules, and one draw needn't show every extreme that they name: `filters`: each channel's filter is a rough sequence times a decay over the lags.
All inputs are finite; a program needn't handle non-finite values.
Results may differ from a plain program's by a relative error of at most 0.013.
Values may be sent and summed in bfloat16 or wider, within the bound.
A program may use at most 128 MiB of HBM per device.

v0:
```python
import math

import jax
import jax.numpy as jnp
from jax import lax
from jax.sharding import PartitionSpec as P

highest = lax.Precision.HIGHEST


def passed_along(value, axis, steps):
    count = lax.axis_size(axis)
    initial, last = (max(0, -steps), min(count, count - steps))
    return lax.ppermute(value, axis, [(source, source + steps) for source in range(initial, last)])


def table(count):
    index = jnp.arange(count, dtype=jnp.int32)
    angle = -2.0 * math.pi / count * (index[:, None] * index[None, :] % count).astype(jnp.float32)
    return (jnp.cos(angle), jnp.sin(angle))


def twiddle(outer, inner, total):
    first = jnp.arange(outer, dtype=jnp.int32)
    second = jnp.arange(inner, dtype=jnp.int32)
    angle = -2.0 * math.pi / total * (first[:, None] * second[None, :] % total).astype(jnp.float32)
    return (jnp.cos(angle), jnp.sin(angle))


def spectrum(field, outer, inner, total):
    outer_re, outer_im = table(outer)
    inner_re, inner_im = table(inner)
    turn_re, turn_im = twiddle(outer, inner, total)
    grid = jnp.pad(field, ((0, 0), (0, total - field.shape[1]))).reshape(
        field.shape[0], outer, inner
    )
    first_re = jnp.einsum("kn,cnm->ckm", outer_re, grid, precision=highest)
    first_im = jnp.einsum("kn,cnm->ckm", outer_im, grid, precision=highest)
    mid_re = first_re * turn_re - first_im * turn_im
    mid_im = first_re * turn_im + first_im * turn_re
    freq_re = jnp.einsum("ckn,nm->ckm", mid_re, inner_re, precision=highest) - jnp.einsum(
        "ckn,nm->ckm", mid_im, inner_im, precision=highest
    )
    freq_im = jnp.einsum("ckn,nm->ckm", mid_re, inner_im, precision=highest) + jnp.einsum(
        "ckn,nm->ckm", mid_im, inner_re, precision=highest
    )
    return (freq_re, freq_im)


def inverse(freq_re, freq_im, outer, inner, total, length):
    outer_re, outer_im = table(outer)
    inner_re, inner_im = table(inner)
    turn_re, turn_im = twiddle(outer, inner, total)
    back_re = jnp.einsum("ckm,nm->ckn", freq_re, inner_re, precision=highest) + jnp.einsum(
        "ckm,nm->ckn", freq_im, inner_im, precision=highest
    )
    back_im = jnp.einsum("ckm,nm->ckn", freq_im, inner_re, precision=highest) - jnp.einsum(
        "ckm,nm->ckn", freq_re, inner_im, precision=highest
    )
    mid_re = back_re * turn_re + back_im * turn_im
    mid_im = back_im * turn_re - back_re * turn_im
    field = jnp.einsum("nk,ckm->cnm", outer_re, mid_re, precision=highest) + jnp.einsum(
        "nk,ckm->cnm", outer_im, mid_im, precision=highest
    )
    return (field / total).reshape(field.shape[0], total)[:, :length]


def on_device(tokens, in_weight, short_taps, filters, cotangent):
    length = filters.shape[1]
    total = 2 * length
    outer = 1
    for factor in range(1, math.isqrt(total) + 1):
        if total % factor == 0:
            outer = factor
    inner = total // outer
    tok_rows = tokens.shape[0]
    gathered = lax.all_gather(tokens, "dp", axis=1, tiled=True)
    projected = jnp.einsum("td,dkc->kct", gathered, in_weight, preferred_element_type=jnp.float32)
    before = passed_along(projected[:, :, tok_rows - 2 :], "context", 1)
    extended = jnp.concatenate([before, projected], axis=2)
    streams = jnp.zeros_like(projected)
    for offset in range(3):
        streams = (
            streams
            + short_taps[:, offset, :, None] * extended[:, :, 2 - offset : 2 - offset + tok_rows]
        )
    gate = streams[0]
    value = streams[1]
    grad_in = cotangent.astype(jnp.float32)
    filt_re, filt_im = spectrum(filters, outer, inner, total)
    value_group = lax.all_to_all(value, "context", split_axis=0, concat_axis=1, tiled=True)
    value_re, value_im = spectrum(value_group, outer, inner, total)
    prod_re = filt_re * value_re - filt_im * value_im
    prod_im = filt_re * value_im + filt_im * value_re
    filtered_group, value_re, value_im = (
        inverse(prod_re, prod_im, outer, inner, total, length),
        value_re,
        value_im,
    )
    filtered = lax.all_to_all(filtered_group, "context", split_axis=1, concat_axis=0, tiled=True)
    output_wide = gate * filtered
    grad_gate = grad_in * filtered
    grad_filtered = grad_in * gate
    grad_group = lax.all_to_all(grad_filtered, "context", split_axis=0, concat_axis=1, tiled=True)
    grad_re, grad_im = spectrum(grad_group, outer, inner, total)
    left_re = filt_re * grad_re + filt_im * grad_im
    left_im = filt_re * grad_im - filt_im * grad_re
    right_re = value_re * grad_re + value_im * grad_im
    right_im = value_re * grad_im - value_im * grad_re
    grad_value = inverse(left_re, left_im, outer, inner, total, length)
    filter_grad = inverse(right_re, right_im, outer, inner, total, length)
    grad_value_group, filter_grad = (grad_value, filter_grad)
    grad_value = lax.all_to_all(
        grad_value_group, "context", split_axis=1, concat_axis=0, tiled=True
    )
    gated_out = output_wide.astype(jnp.bfloat16)
    grad_streams = jnp.stack([grad_gate, grad_value])
    after = passed_along(grad_streams[:, :, :2], "context", -1)
    grad_extended = jnp.concatenate([grad_streams, after], axis=2)
    proj_wide = jnp.zeros_like(grad_streams)
    for offset in range(3):
        proj_wide = (
            proj_wide
            + short_taps[:, offset, :, None] * grad_extended[:, :, offset : offset + tok_rows]
        )
    proj_grad = proj_wide.astype(jnp.bfloat16)
    partial_value = jnp.einsum(
        "kct,dkc->td", proj_grad, in_weight, preferred_element_type=jnp.float32
    )
    token_grad = lax.psum_scatter(
        partial_value.astype(jnp.bfloat16), "dp", scatter_dimension=1, tiled=True
    )
    weight_wide = lax.psum_scatter(
        jnp.einsum("td,kct->dkc", gathered, proj_grad, preferred_element_type=jnp.float32),
        "context",
        scatter_dimension=0,
        tiled=True,
    )
    return (gated_out, token_grad, weight_wide.astype(jnp.bfloat16), filter_grad)


def solution(mesh):
    placed = (
        P("context", "dp"),
        P(None, None, "dp"),
        P(None, None, "dp"),
        P(("dp", "context"), None),
        P("dp", "context"),
    )
    return jax.shard_map(
        on_device,
        mesh=mesh,
        in_specs=placed,
        out_specs=(
            P("dp", "context"),
            P("context", "dp"),
            P("context", None, "dp"),
            P(("dp", "context"), None),
        ),
        check_vma=False,
    )
```

profile of v0, /device:TPU:0, one launch (start us, length us, event | category | flops | bytes accessed | tf_op | source)
XLA Modules:
  0.0 925.6 jit_solution(3245116032578762829)
XLA Ops:
  7.9 1.0 pad_bitcast_fusion.2
  9.2 0.7 convolution_bitcast_fusion.5
  9.9 0.7 convolution_bitcast_fusion.6
  10.6 0.8 fusion.60
  11.5 0.8 fusion.61
  12.3 0.8 convolution_add_fusion.8
  13.1 25.7 %all-gather.2.cloned.1.call-done = bf16[128,8192]{1,0:T(8,128)(2,1)} async-done(((bf16[128,2048]{1,0:T(8,128)(2,1)}), bf16[128,8192]{1,0:T(8,128)(2,1)}) %all-gather.2.cloned.1.call-update) | async-done | bytes 2097168 | tf_op jit(solution)/shard_map/all_gather | solution.py:77
  38.8 10.5 %fusion = f32[2,512,128]{2,1,0:T(8,128)S(1)} fusion(bf16[8192,2,512]{2,1,0:T(2,128)(2,1)} %param.6, bf16[128,8192]{1,0:T(8,128)(2,1)} %all-gather.2.cloned.1.call-done), kind=kOutput, calls=%fused_computation.1 | convolution fusion | flops 2147483648 | bytes 19398656 | tf_op jit(solution)/shard_map/td,dkc->kct/dot_general | solution.py:78
  49.5 2.5 collective-permute-start
  52.1 11.5 %collective-permute-done = f32[2,512,2]{2,1,0:T(8,128)S(1)} collective-permute-done((f32[2,512,2]{2,1,0:T(8,128)S(1)}, f32[2,512,2]{2,1,0:T(8,128)S(1)}, u32[]{:S(2)}, u32[]{:S(2)}) %collective-permute-start) | collective-permute-done | bytes 8224 | tf_op jit(solution)/shard_map/ppermute | solution.py:14
  63.6 0.9 fusion.23
  64.5 0.7 convert_multiply_fusion
  65.2 10.0 %all-to-all-start.2 = ((f32[32,16,128]{2,1,0:T(8,128)}), f32[32,16,128]{2,1,0:T(8,128)S(1)}, u32[]{:S(2)}, u32[]{:S(2)}) async-start(f32[32,16,128]{2,1,0:T(8,128)} %bitcast.20), calls=%async_computation.2 | async-start | bytes 524288 | tf_op jit(solution)/shard_map/all_to_all | solution.py:104
  75.2 0.8 convolution_subtract_fusion.5
  76.1 0.7 slice.63
  76.8 7.9 all-to-all-done.2
  84.7 4.0 all-to-all-start
  88.9 0.7 convolution_bitcast_fusion.1
  89.6 0.7 convolution_bitcast_fusion.2
  90.4 7.6 all-to-all-done
  98.1 0.7 convolution_bitcast_fusion.3
  98.9 0.7 convolution_bitcast_fusion.4
  99.6 0.8 fusion.65
  100.4 0.8 fusion.64
  101.3 0.8 fusion.63
  102.1 0.8 fusion.62
  102.9 0.8 convolution_subtract_fusion.2
  103.8 0.8 convolution_subtract_fusion.4
  104.6 0.8 convolution_add_fusion.4
  105.4 1.1 multiply_add_fusion
  106.5 0.8 fusion.87
  107.4 0.8 fusion.85
  108.2 1.0 convolution_add_fusion.3
  109.2 0.8 convolution_subtract_fusion.1
  110.1 0.8 fusion.93
  110.9 0.8 fusion.91
  111.7 0.8 convolution_add_fusion.6
  112.5 0.8 convolution_subtract_fusion.3
  113.4 0.8 fusion.42
  114.2 0.8 fusion.14
  115.3 0.7 copy_bitcast_fusion.6
  116.0 3.9 all-to-all-start.1
  119.9 0.8 fusion.35
  120.7 0.8 fusion.13
  121.8 0.7 copy_bitcast_fusion.5
  122.5 6.8 all-to-all-done.1
  129.3 3.9 all-to-all-start.3
  133.9 8.8 all-to-all-done.3
  142.7 1.3 collective-permute-start.1
  144.0 9.8 %collective-permute-done.1 = f32[2,512,2]{2,1,0:T(8,128)S(1)} collective-permute-done((f32[2,512,2]{2,1,0:T(8,128)S(1)}, f32[2,512,2]{2,1,0:T(8,128)S(1)}, u32[]{:S(2)}, u32[]{:S(2)}) %collective-permute-start.1) | collective-permute-done | bytes 8224 | tf_op jit(solution)/shard_map/ppermute | solution.py:14
  153.9 0.7 fusion.19
  154.6 14.9 %convolution_bitcast_fusion = f32[8192,2,512]{0,2,1:T(8,128)} fusion(bf16[2,512,128]{2,1,0:T(8,128)(2,1)S(1)} %fusion.19, bf16[128,8192]{1,0:T(8,128)(2,1)} %all-gather.2.cloned.1.call-done), kind=kOutput, calls=%fused_computation | convolution fusion | flops 2147483648 | bytes 35913728 | tf_op jit(solution)/shard_map/td,kct->dkc/dot_general | solution.py:134
  169.6 12.8 %fusion.7 = bf16[128,8192]{1,0:T(8,128)(2,1)} fusion(bf16[2,512,128]{2,1,0:T(8,128)(2,1)S(1)} %fusion.19, bf16[8192,2,512]{2,1,0:T(2,128)(2,1)} %param.6), kind=kOutput, calls=%fused_computation.6 | convolution fusion | flops 2148532224 | bytes 19136512 | tf_op jit(solution)/shard_map/kct,dkc->td/dot_general | solution.py:127
  182.5 0.8 fusion.83
  183.3 0.8 fusion.81
  184.1 0.8 convolution_add_fusion.1
  185.0 0.8 convolution_subtract_fusion
  185.8 0.8 fusion.28
  186.6 0.8 fusion.12
  187.7 0.7 slice.70
  188.4 687.7 %reduce-scatter.5.cloned.1.call-done = f32[256,2,512]{0,2,1:T(8,128)} async-done(((f32[8192,2,512]{0,2,1:T(8,128)}), f32[256,2,512]{0,2,1:T(8,128)}) %reduce-scatter.5.cloned.1.call-update) | async-done | bytes 1048592 | tf_op jit(solution)/shard_map/reduce_scatter | solution.py:133
  876.1 1.3 convert_element_type.171
  877.3 1.2 copy.28
  878.5 40.1 %reduce-scatter.3.cloned.1.call-done = bf16[128,2048]{1,0:T(8,128)(2,1)} async-done(((bf16[128,8192]{1,0:T(8,128)(2,1)}), bf16[128,2048]{1,0:T(8,128)(2,1)}) %reduce-scatter.3.cloned.1.call-update) | async-done | bytes 524304 | tf_op jit(solution)/shard_map/reduce_scatter | solution.py:130
  (28 shorter events, 3.3 us)
Async XLA Ops:
  7.2 31.6 %all-gather.2.cloned.1.call-start = ((), (), s32[]{:S(2)}) async-start(), calls=%async_computation.6 | async-start | bytes 2621440 | tf_op jit(solution)/shard_map/all_gather | solution.py:77
  11.5 40.6 %copy-start.2 = (f32[2,3,512]{2,0,1:T(2,128)S(1)}, f32[2,3,512]{2,0,1:T(2,128)}, u32[]{:S(2)}) copy-start(f32[2,3,512]{2,0,1:T(2,128)} %param.7) | copy-start | bytes 36868
  12.3 52.2 %copy-start = (bf16[512,128]{1,0:T(8,128)(2,1)S(1)}, bf16[512,128]{1,0:T(8,128)(2,1)}, u32[]{:S(2)}) copy-start(bf16[512,128]{1,0:T(8,128)(2,1)} %param.9) | copy-start | bytes 393220
  49.5 14.1 %collective-permute-start = (f32[2,512,2]{2,1,0:T(8,128)S(1)}, f32[2,512,2]{2,1,0:T(8,128)S(1)}, u32[]{:S(2)}, u32[]{:S(2)}) collective-permute-start(f32[2,512,2]{2,1,0:T(8,128)S(1)} %slice.59), channel_id=1, source_target_pairs={{0,1},{1,2},{2,3},{3,4},{4,5},{5,6},{6,7},{7,8},{8,9},{9,10},{10,1... | collective-permute-start | bytes 24584 | tf_op jit(solution)/shard_map/ppermute | solution.py:14
  65.2 19.5 %all-to-all-start.2 = ((f32[32,16,128]{2,1,0:T(8,128)}), f32[32,16,128]{2,1,0:T(8,128)S(1)}, u32[]{:S(2)}, u32[]{:S(2)}) async-start(f32[32,16,128]{2,1,0:T(8,128)} %bitcast.20), calls=%async_computation.2 | async-start | bytes 524288 | tf_op jit(solution)/shard_map/all_to_all | solution.py:104
  84.7 13.3 %all-to-all-start = ((f32[32,16,128]{2,1,0:T(8,128)}), f32[32,16,128]{2,1,0:T(8,128)S(1)}, u32[]{:S(2)}, u32[]{:S(2)}) async-start(f32[32,16,128]{2,1,0:T(8,128)} %bitcast.11), calls=%async_computation | async-start | bytes 524288 | tf_op jit(solution)/shard_map/all_to_all | solution.py:91
  103.8 29.4 %copy-start.1 = (bf16[512,128]{1,0:T(8,128)(2,1)S(1)}, bf16[512,128]{1,0:T(8,128)(2,1)}, u32[]{:S(2)}) copy-start(bf16[512,128]{1,0:T(8,128)(2,1)} %param.9) | copy-start | bytes 393220
  116.0 13.3 %all-to-all-start.1 = ((f32[16,32,128]{2,0,1:T(8,128)}), f32[16,32,128]{2,0,1:T(8,128)S(1)}, u32[]{:S(2)}, u32[]{:S(2)}) async-start(f32[16,32,128]{2,0,1:T(8,128)} %copy_bitcast_fusion.6), calls=%async_computation.1 | async-start | bytes 524288 | tf_op jit(solution)/shard_map/all_to_all | solution.py:100
  129.3 13.4 %all-to-all-start.3 = ((f32[16,32,128]{2,0,1:T(8,128)}), f32[16,32,128]{2,0,1:T(8,128)S(1)}, u32[]{:S(2)}, u32[]{:S(2)}) async-start(f32[16,32,128]{2,0,1:T(8,128)} %copy_bitcast_fusion.5), calls=%async_computation.3 | async-start | bytes 524288 | tf_op jit(solution)/shard_map/all_to_all | solution.py:113
  133.2 742.9 %reduce-scatter.5.cloned.1.call-start = ((), (), s32[]{:S(2)}) async-start(), calls=%async_computation.8 | async-start | bytes 34603008 | tf_op jit(solution)/shard_map/reduce_scatter | solution.py:133
  142.7 11.1 %collective-permute-start.1 = (f32[2,512,2]{2,1,0:T(8,128)S(1)}, f32[2,512,2]{2,1,0:T(8,128)S(1)}, u32[]{:S(2)}, u32[]{:S(2)}) collective-permute-start(f32[2,512,2]{2,1,0:T(8,128)S(1)} %fusion.15), channel_id=1, source_target_pairs={{1,0},{2,1},{3,2},{4,3},{5,4},{6,5},{7,6},{8,7},{9,8},{10,9},{11,1... | collective-permute-start | bytes 24584 | tf_op jit(solution)/shard_map/ppermute | solution.py:14
  169.6 749.0 %reduce-scatter.3.cloned.1.call-start = ((), (), s32[]{:S(2)}) async-start(), calls=%async_computation.7 | async-start | bytes 2621440 | tf_op jit(solution)/shard_map/reduce_scatter | solution.py:130
Sparse Core Ops, SparseCore 0:
  9.7 29.0 all-gather.1
  169.7 706.2 reduce-scatter.4
  879.3 39.3 reduce-scatter.2
where the time goes:
time: 934 us; the launch traced here: 926 us
  waiting for transfers between devices  806 us (86%)
  matrix products  67.5 us (7%)
  starting transfers between devices  25.7 us (3%)
  between operations  14.7 us (2%)
    reduce_scatter x1, waiting for transfers between devices, on_device(): lax.psum_scatter(jnp.einsum('td,kct->dkc', gathered, proj_grad, preferred...  688 us
    reduce_scatter x1, waiting for transfers between devices, on_device(): lax.psum_scatter(partial_value.astype(jnp.bfloat16), 'dp', scatter_dimens...  40.1 us
    all_gather x1, waiting for transfers between devices, on_device(): gathered = lax.all_gather(tokens, 'dp', axis=1, tiled=True)  25.7 us
    ppermute x2, waiting for transfers between devices, passed_along(): lax.ppermute(value, axis, [(source, source + steps) for source in range(i...  21.3 us
  transfers between devices with their start and end apart: 9, of which 9 were waited for; matrix products, arithmetic and copies ran while one was open for 4% of the time, Pallas kernels for 0%

commit v1 on v0

v1 whole, which is shorter than its diff:
```python
import functools
import math

import jax
import jax.numpy as jnp
import numpy as np
from jax import lax
from jax.experimental import pallas as pl
from jax.experimental.pallas import tpu as pltpu
from jax.sharding import PartitionSpec as P

OUTER = 64
INNER = 128
TOTAL = OUTER * INNER
HALF = OUTER // 2
KEPT = [0, 8, 16, 24, 32] + [k1 + 8 * k2 for k1 in (1, 2, 3) for k2 in range(8)] + [4, 12, 20, 28]
ROWS = len(KEPT)


def add(a, b):
    return b if a is None else a if b is None else a + b


def neg(a):
    return None if a is None else -a


def sub(a, b):
    return a if b is None else neg(b) if a is None else a - b


def scaled(a, factor):
    if a is None or abs(factor) < 1e-12:
        return None
    if abs(factor - 1) < 1e-12:
        return a
    if abs(factor + 1) < 1e-12:
        return -a
    return a * np.float32(factor)


def cadd(a, b):
    return (add(a[0], b[0]), add(a[1], b[1]))


def csub(a, b):
    return (sub(a[0], b[0]), sub(a[1], b[1]))


def turned(a, step, count):
    step %= count
    if (8 * step) % count == 0 and (8 * step // count) % 2 == 1:
        eighth = 8 * step // count
        root = math.sqrt(0.5)
        re, im = a
        if eighth == 1:
            pair = (sub(re, im), add(re, im))
        elif eighth == 3:
            pair = (neg(add(re, im)), sub(re, im))
        elif eighth == 5:
            pair = (sub(im, re), neg(add(re, im)))
        else:
            pair = (add(re, im), sub(im, re))
        return (scaled(pair[0], root), scaled(pair[1], root))
    angle = 2 * math.pi * step / count
    cos, sin = math.cos(angle), math.sin(angle)
    return (
        sub(scaled(a[0], cos), scaled(a[1], sin)),
        add(scaled(a[0], sin), scaled(a[1], cos)),
    )


def dft(values, sign):
    count = len(values)
    if count == 1:
        return values
    even = dft(values[0::2], sign)
    odd = dft(values[1::2], sign)
    odd = [turned(entry, sign * index, count) for index, entry in enumerate(odd)]
    return [cadd(a, b) for a, b in zip(even, odd)] + [csub(a, b) for a, b in zip(even, odd)]


def outer_forward(load):
    parts = []
    for second in range(8):
        line = [(load(8 * first + second), None) if first < 4 else (None, None) for first in range(8)]
        parts.append(dft(line, -1)[:5])
    results = []
    for first in (0, 1, 2, 3, 4):
        line = [turned(parts[second][first], -second * first, OUTER) for second in range(8)]
        full = dft(line, -1)
        results += {0: full[:5], 4: full[:4]}.get(first, full)
    return results


def real_sum(values, index):
    total = None
    for j, entry in enumerate(values):
        total = add(total, turned(entry, j * index, 8)[0])
    return total


def real_line(values, count):
    top = values[0][0]
    last = values[4][0]
    a = add(top, last)
    b = sub(top, last)
    (r1, i1), (r2, i2), (r3, i3) = values[1:4]
    s13, d13 = add(r1, r3), sub(r1, r3)
    si, di = add(i1, i3), sub(i1, i3)
    root = math.sqrt(0.5)
    p = scaled(sub(d13, si), root)
    q = scaled(add(d13, si), root)
    out = [
        add(add(a, r2), s13),
        add(sub(b, i2), p),
        sub(sub(a, r2), di),
        sub(add(b, i2), q),
    ]
    if count > 4:
        out += [
            sub(add(a, r2), s13),
            sub(sub(b, i2), p),
            add(sub(a, r2), di),
            add(add(b, i2), q),
        ]
    return out


def outer_inverse(load):
    zero = real_line([load(row) for row in range(5)], 8)
    lines = []
    for first in (1, 2, 3):
        line = dft([load(5 + 8 * (first - 1) + second) for second in range(8)], 1)
        lines.append([turned(line[second], second * first, OUTER) for second in range(8)])
    tail = dft([load(29 + second) if second < 4 else (None, None) for second in range(8)], 1)
    tail = [turned(tail[second], second, 16)[0] for second in range(8)]
    results = [None] * HALF
    for second in range(8):
        line = [(zero[second], None)] + [lines[first][second] for first in range(3)] + [(tail[second], None)]
        for first, entry in enumerate(real_line(line, 4)):
            results[8 * first + second] = entry
    return results


def tables():
    index = np.arange(INNER, dtype=np.float64)
    angle = 2 * np.pi / INNER * (np.outer(index, index) % INNER)
    cos, sin = np.cos(angle), np.sin(angle)
    wide = np.block([[cos, -sin], [sin, cos]])
    high = wide.astype(jnp.bfloat16)
    low = (wide - high.astype(np.float64)).astype(jnp.bfloat16)
    inverse = wide.T
    inverse_high = inverse.astype(jnp.bfloat16)
    inverse_low = (inverse - inverse_high.astype(np.float64)).astype(jnp.bfloat16)
    matrices = np.stack([high, low, inverse_high, inverse_low])
    turn = 2 * np.pi / TOTAL * np.outer(np.array(KEPT, np.float64), index)
    weight = np.array([1.0 if k in (0, HALF) else 2.0 for k in KEPT])[:, None] / TOTAL
    turns = np.stack([np.cos(turn), np.sin(turn), weight * np.cos(turn), weight * np.sin(turn)])
    return matrices, turns.astype(np.float32)


def times_matrix(wide, high, low):
    top = wide.astype(jnp.bfloat16)
    rest = (wide - top.astype(jnp.float32)).astype(jnp.bfloat16)
    dot = functools.partial(jnp.dot, preferred_element_type=jnp.float32)
    return dot(top, high) + (dot(rest, high) + dot(top, low))


def lagged(here, before, lag):
    lane = lax.broadcasted_iota(jnp.int32, here.shape, here.ndim - 1)
    rolled = pltpu.roll(here, lag, here.ndim - 1)
    if before is None:
        return jnp.where(lane < lag, 0.0, rolled)
    return jnp.where(lane < lag, pltpu.roll(before, lag, here.ndim - 1), rolled)


def led(here, after, lead):
    lane = lax.broadcasted_iota(jnp.int32, here.shape, here.ndim - 1)
    width = here.shape[-1]
    rolled = pltpu.roll(here, width - lead, here.ndim - 1)
    if after is None:
        return jnp.where(lane >= width - lead, 0.0, rolled)
    return jnp.where(lane >= width - lead, pltpu.roll(after, width - lead, here.ndim - 1), rolled)


def conv_kernel(
    proj_ref, cot_ref, filt_ref, taps_ref, mat_ref, turn_ref,
    back_ref, pair_ref, fgrad_ref,
    gate_ref, value_ref, gfilt_ref, gval_ref, spec_ref, prod_ref,
):
    channels = filt_ref.shape[0]

    def short(stream, n):
        here = proj_ref[n, stream].astype(jnp.float32)
        before = proj_ref[n - 1, stream].astype(jnp.float32) if n else None
        total = taps_ref[stream, 0] * here
        for lag in (1, 2):
            total = total + taps_ref[stream, lag] * lagged(here, before, lag)
        return total

    for n in range(HALF):
        gate = short(0, n)
        gate_ref[n] = gate
        gfilt_ref[n] = cot_ref[n].astype(jnp.float32) * gate
        value_ref[n] = short(1, n)

    sources = (
        lambda n: filt_ref[:, n * INNER : (n + 1) * INNER],
        lambda n: value_ref[n],
        lambda n: gfilt_ref[n],
    )
    for which, load in enumerate(sources):
        for row, (re, im) in enumerate(outer_forward(load)):
            cos = turn_ref[0, row][None, :]
            sin = turn_ref[1, row][None, :]
            at = pl.ds((which * ROWS + row) * channels, channels)
            if im is None:
                spec_ref[at, :INNER] = re * cos
                spec_ref[at, INNER:] = -(re * sin)
            else:
                spec_ref[at, :INNER] = re * cos + im * sin
                spec_ref[at, INNER:] = im * cos - re * sin
    size = ROWS * channels
    for which in range(3):
        at = pl.ds(which * size, size)
        spec_ref[at, :] = times_matrix(spec_ref[at, :], mat_ref[0], mat_ref[1])

    @pl.loop(0, ROWS)
    def _(row):
        def part(which):
            at = pl.ds(pl.multiple_of((which * ROWS + row) * channels, channels), channels)
            return spec_ref[at, :INNER], spec_ref[at, INNER:]

        (hr, hi), (vr, vi), (gr, gi) = part(0), part(1), part(2)

        def put(which, re, im):
            at = pl.ds(pl.multiple_of((which * ROWS + row) * channels, channels), channels)
            prod_ref[at, :INNER] = re
            prod_ref[at, INNER:] = im

        put(0, hr * vr - hi * vi, hr * vi + hi * vr)
        put(1, hr * gr + hi * gi, hr * gi - hi * gr)
        put(2, vr * gr + vi * gi, vr * gi - vi * gr)

    for which in range(3):
        at = pl.ds(which * size, size)
        prod_ref[at, :] = times_matrix(prod_ref[at, :], mat_ref[2], mat_ref[3])

    def turned_row(which):
        def load(row):
            cos = turn_ref[2, row][None, :]
            sin = turn_ref[3, row][None, :]
            at = pl.ds((which * ROWS + row) * channels, channels)
            re, im = prod_ref[at, :INNER], prod_ref[at, INNER:]
            return re * cos - im * sin, im * cos + re * sin

        return load

    for n, entry in enumerate(outer_inverse(turned_row(0))):
        back_ref[n, 2] = (gate_ref[n] * entry).astype(back_ref.dtype)
        gate_ref[n] = cot_ref[n].astype(jnp.float32) * entry
    for n, entry in enumerate(outer_inverse(turned_row(1))):
        gval_ref[n] = entry
    for n, entry in enumerate(outer_inverse(turned_row(2))):
        fgrad_ref[:, n * INNER : (n + 1) * INNER] = entry

    for stream, ref in enumerate((gate_ref, gval_ref)):
        for n in range(HALF):
            here = ref[n]
            after = ref[n + 1] if n + 1 < HALF else None
            total = taps_ref[stream, 0] * here
            for lead in (1, 2):
                total = total + taps_ref[stream, lead] * led(here, after, lead)
            total = total.astype(jnp.bfloat16)
            back_ref[n, stream] = total
            pair_ref[stream, :, n * INNER : (n + 1) * INNER] = total


def convolved(projected, cotangent, filters, taps):
    channels, length = filters.shape
    matrices, turns = tables()
    f32 = functools.partial(pltpu.VMEM, dtype=jnp.float32)
    return pl.pallas_call(
        conv_kernel,
        out_shape=(
            jax.ShapeDtypeStruct((HALF, 3, channels, INNER), jnp.bfloat16),
            jax.ShapeDtypeStruct((2, channels, length), jnp.bfloat16),
            jax.ShapeDtypeStruct((channels, length), jnp.float32),
        ),
        in_specs=[pl.BlockSpec(memory_space=pltpu.VMEM)] * 6,
        out_specs=[pl.BlockSpec(memory_space=pltpu.VMEM)] * 3,
        scratch_shapes=[
            f32((HALF, channels, INNER)),
            f32((HALF, channels, INNER)),
            f32((HALF, channels, INNER)),
            f32((HALF, channels, INNER)),
            f32((3 * ROWS * channels, 2 * INNER)),
            f32((3 * ROWS * channels, 2 * INNER)),
        ],
        compiler_params=pltpu.CompilerParams(vmem_limit_bytes=32 * 1024 * 1024),
        cost_estimate=pl.CostEstimate(flops=1_300_000_000, bytes_accessed=2_000_000, transcendentals=0),
        name="long_convolutions",
    )(projected, cotangent, filters, taps, jnp.asarray(matrices), jnp.asarray(turns))


def on_device(tokens, in_weight, short_taps, filters, cotangent):
    channels, length = filters.shape
    groups = lax.axis_size("context")
    rows = tokens.shape[0]
    slab = in_weight.shape[2]
    gathered = lax.all_gather(tokens, "dp", axis=1, tiled=True)
    cot_group = lax.all_to_all(
        cotangent.reshape(groups, channels, rows), "context", split_axis=0, concat_axis=0, tiled=True
    )
    projected = jnp.einsum("td,dkc->kct", gathered, in_weight, preferred_element_type=jnp.float32)
    outgoing = projected.astype(jnp.bfloat16).reshape(2, groups, channels, rows).transpose(1, 0, 2, 3)
    proj_group = lax.all_to_all(outgoing, "context", split_axis=0, concat_axis=0, tiled=True)
    own = lax.dynamic_slice_in_dim(short_taps, lax.axis_index("context") * channels, channels, axis=2)
    taps = jnp.broadcast_to(own[..., None], own.shape + (INNER,))
    back, pair, filter_grad = convolved(proj_group, cot_group, filters, taps)
    back = lax.all_to_all(back, "context", split_axis=0, concat_axis=0, tiled=True)
    gated_out = back[:, 2].reshape(slab, rows)
    proj_grad = back[:, :2].transpose(1, 0, 2, 3).reshape(2, slab, rows)
    partial_value = jnp.einsum("kct,dkc->td", proj_grad, in_weight, preferred_element_type=jnp.float32)
    token_grad = lax.psum_scatter(
        partial_value.astype(jnp.bfloat16), "dp", scatter_dimension=1, tiled=True
    )
    tokens_own = lax.all_to_all(gathered, "context", split_axis=1, concat_axis=0, tiled=True)
    whole = lax.all_gather(pair, "context", axis=0, tiled=False)
    weight_grad = jnp.einsum("td,gkct->dkgc", tokens_own, whole, preferred_element_type=jnp.float32)
    weight_grad = weight_grad.astype(jnp.bfloat16).reshape(tokens_own.shape[1], 2, slab)
    return (gated_out, token_grad, weight_grad, filter_grad)


def solution(mesh):
    placed = (
        P("context", "dp"),
        P(None, None, "dp"),
        P(None, None, "dp"),
        P(("dp", "context"), None),
        P("dp", "context"),
    )
    return jax.shard_map(
        on_device,
        mesh=mesh,
        in_specs=placed,
        out_specs=(
            P("dp", "context"),
            P("context", "dp"),
            P("context", None, "dp"),
            P(("dp", "context"), None),
        ),
        check_vma=False,
    )
```

time: 934 us -> 332 us (0.36)
  waiting for transfers between devices: 806 us -> 241 us
  matrix products: 67.5 us -> 29.7 us
  blocking collectives: 0 us -> 16.9 us
    reduce_scatter x1 -> x0, waiting for transfers between devices: 688 us -> none  [on_device(): lax.psum_scatter(jnp.einsum('td,kct->dkc', gathered, proj_grad, preferred...]
    all_gather x0 -> x1, waiting for transfers between devices: none -> 142 us  [on_device(): whole = lax.all_gather(pair, 'context', axis=0, tiled=False)]
    dot_general x37 -> x1, matrix products: 44.2 us -> 5.72 us  [on_device(): jnp.einsum('td,gkct->dkgc', tokens_own, whole, preferred_element_type=jnp...]
    ppermute x2 -> x0, waiting for transfers between devices: 21.3 us -> none  [passed_along(): lax.ppermute(value, axis, [(source, source + steps) for source in range(i...]
    all_to_all x0 -> x1, blocking collectives: none -> 16.9 us  [on_device(): lax.all_to_all(back, 'context', split_axis=0, concat_axis=0, tiled=True)]
    all_to_all x4 -> x3, waiting for transfers between devices: 31 us -> 44.8 us  [the longest x1 35.1 us: on_device(): lax.all_to_all(gathered, 'context', split_axis=1, concat_axis=0, tiled=True)]
    all_to_all x4 -> x3, starting transfers between devices: 21.8 us -> 20.7 us  [the longest x1 9.27 us: on_device(): lax.all_to_all(cotangent.reshape(groups, channels, rows), 'context', spli...]
  transfers between devices with their start and end apart: 9 -> 6, of which waited for: 9 -> 5; matrix products, arithmetic and copies ran while one was open for 4% -> 10% of each run, Pallas kernels for 0% -> 0%
where the time goes in v1:
time: 332 us; the launch traced here: 331 us
  waiting for transfers between devices  241 us (73%)
  matrix products  29.7 us (9%)
  starting transfers between devices  20.8 us (6%)
  blocking collectives  16.9 us (5%)
  between operations  13.9 us (4%)
  local copies, waits for them, and re-layouts  4.41 us (1%)
  Pallas kernels  4.26 us (1%)
    all_gather x1, waiting for transfers between devices, on_device(): whole = lax.all_gather(pair, 'context', axis=0, tiled=False)  142 us
    all_to_all x1, waiting for transfers between devices, on_device(): lax.all_to_all(gathered, 'context', split_axis=1, concat_axis=0, tiled=True)  35.1 us
    reduce_scatter x1, waiting for transfers between devices, on_device(): lax.psum_scatter(partial_value.astype(jnp.bfloat16), 'dp', scatter_dimens...  32.1 us
    all_gather x1, waiting for transfers between devices, on_device(): gathered = lax.all_gather(tokens, 'dp', axis=1, tiled=True)  21.6 us
    all_to_all x1, blocking collectives, on_device(): lax.all_to_all(back, 'context', split_axis=0, concat_axis=0, tiled=True)  16.9 us
    dot_general x1, matrix products, on_device(): jnp.einsum('kct,dkc->td', proj_grad, in_weight, preferred_element_type=jn...  13.1 us
    dot_general x1, matrix products, on_device(): jnp.einsum('td,dkc->kct', gathered, in_weight, preferred_element_type=jnp...  10.9 us
    all_to_all x1, waiting for transfers between devices, on_device(): lax.all_to_all(outgoing, 'context', split_axis=0, concat_axis=0, tiled=True)  9.65 us
  transfers between devices with their start and end apart: 6, of which 5 were waited for; matrix products, arithmetic and copies ran while one was open for 10% of the time, Pallas kernels for 0%

profile of v1, /device:TPU:0, one launch (start us, length us, event | category | flops | bytes accessed | tf_op | source)
XLA Modules:
  0.0 331.3 jit_solution(14595913377913290975)
XLA Ops:
  7.2 0.0 copy-start
  7.2 0.0 all-gather.4.cloned.1.call-start
  7.2 0.7 all-gather.4.cloned.1.call-update
  7.9 9.3 %all-to-all-start.1 = ((bf16[32,16,128]{2,1,0:T(8,128)(2,1)}), bf16[32,16,128]{2,1,0:T(8,128)(2,1)S(1)}, u32[]{:S(2)}, u32[]{:S(2)}) async-start(bf16[32,16,128]{2,1,0:T(8,128)(2,1)} %bitcast.41), calls=%async_computation.1 | async-start | bytes 262144 | tf_op jit(solution)/shard_map/all_to_all | solution.py:313
  17.2 0.0 copy-start.1
  17.2 0.0 copy-start.2
  17.2 0.0 copy-start.3
  17.2 21.6 %all-gather.4.cloned.1.call-done = bf16[128,8192]{1,0:T(8,128)(2,1)} async-done(((bf16[128,2048]{1,0:T(8,128)(2,1)}), bf16[128,8192]{1,0:T(8,128)(2,1)}) %all-gather.4.cloned.1.call-update) | async-done | bytes 2097168 | tf_op jit(solution)/shard_map/all_gather | solution.py:312
  38.8 10.9 %fusion.12 = bf16[2,512,128]{2,1,0:T(8,128)(2,1)S(1)} fusion(bf16[128,8192]{1,0:T(8,128)(2,1)} %all-gather.4.cloned.1.call-done, bf16[8192,2,512]{2,1,0:T(2,128)(2,1)} %param.8), kind=kOutput, calls=%fused_computation.10 | convolution fusion | flops 2147614720 | bytes 19136512 | tf_op jit(solution)/shard_map/td,dkc->kct/dot_general | solution.py:316
  49.7 0.7 copy.49
  50.5 0.0 all-to-all-done.1.cot_ref
  50.5 7.3 %all-to-all-start = ((bf16[32,2,16,128]{3,2,1,0:T(8,128)(2,1)}), bf16[32,2,16,128]{3,2,1,0:T(8,128)(2,1)S(1)}, u32[]{:S(2)}, u32[]{:S(2)}) async-start(bf16[32,2,16,128]{3,2,1,0:T(8,128)(2,1)} %bitcast.35), calls=%async_computation | async-start | bytes 524288 | tf_op jit(solution)/shard_map/all_to_all | solution.py:318
  57.7 0.0 all-gather.6.cloned.1.call-start
  57.8 0.0 copy-done
  57.8 0.1 constant_dynamic-slice_fusion
  57.9 9.7 %all-to-all-done.proj_ref = bf16[32,2,16,128]{3,2,1,0:T(8,128)(2,1)S(1)} async-done(((bf16[32,2,16,128]{3,2,1,0:T(8,128)(2,1)}), bf16[32,2,16,128]{3,2,1,0:T(8,128)(2,1)S(1)}, u32[]{:S(2)}, u32[]{:S(2)}) %all-to-all-start) | async-done | bytes 262176 | tf_op jit(solution)/shard_map/all_to_all | solution.py:318
  67.5 0.1 broadcast_in_dim.2.taps_ref
  67.6 0.0 copy-done.1
  67.6 0.0 copy-done.2
  67.6 0.0 copy-done.3
  67.6 4.3 %long_convolutions.1 = (bf16[32,3,16,128]{3,2,1,0:T(8,128)(2,1)S(1)}, bf16[2,16,4096]{2,1,0:T(8,128)(2,1)}, f32[16,4096]{1,0:T(8,128)}) custom-call(bf16[32,2,16,128]{3,2,1,0:T(8,128)(2,1)S(1)} %all-to-all-done.proj_ref, bf16[32,16,128]{2,1,0:T(8,128)(2,1)S(1)} %all-to-all-done.1.cot_ref, f32[16,4096]{1,0:T(8,128)S(1)} %copy-done.1, ...), custom_call_target="tpu_custom_call" | custom-call | flops 1300000000 | bytes 2000000 | tf_op jit(solution)/shard_map/long_convolutions/pallas_call | solution.py:284
  71.9 0.0 all-gather.6.cloned.1.call-update
  71.9 0.0 reduce-scatter.2.cloned.1.call-start
  71.9 16.9 %all_to_all.34 = bf16[32,3,16,128]{3,2,1,0:T(8,128)(2,1)S(1)} all-to-all(bf16[32,3,16,128]{3,2,1,0:T(8,128)(2,1)S(1)} %get-tuple-element.7), channel_id=1, replica_groups=mesh['dp'=4,'context'=32] {'context'}, dimensions={0} | all-to-all | bytes 786432 | tf_op jit(solution)/shard_map/all_to_all | solution.py:322
  88.9 0.0 copy-start.4
  88.9 13.1 %fusion.7 = bf16[128,8192]{1,0:T(8,128)(2,1)} fusion(bf16[2,512,128]{2,1,0:T(8,128)(2,1)S(1)} %bitcast.39, bf16[8192,2,512]{2,1,0:T(2,128)(2,1)} %param.8), kind=kOutput, calls=%fused_computation.5 | convolution fusion | flops 2148532224 | bytes 19136512 | tf_op jit(solution)/shard_map/kct,dkc->td/dot_general | solution.py:325
  102.0 0.0 reduce-scatter.2.cloned.1.call-update
  102.0 0.0 copy-done.4
  102.0 1.6 copy.48
  103.6 4.2 %all-to-all-start.3 = ((bf16[128,32,256]{2,0,1:T(8,128)(2,1)}), bf16[128,32,256]{2,0,1:T(8,128)(2,1)S(1)}, u32[]{:S(2)}, u32[]{:S(2)}) async-start(bf16[128,32,256]{2,0,1:T(8,128)(2,1)} %bitcast.34), calls=%async_computation.4 | async-start | bytes 4194304 | tf_op jit(solution)/shard_map/all_to_all | solution.py:329
  107.8 0.7 slice.8
  108.4 35.1 %all-to-all-done.3 = bf16[128,32,256]{2,0,1:T(8,128)(2,1)S(1)} async-done(((bf16[128,32,256]{2,0,1:T(8,128)(2,1)}), bf16[128,32,256]{2,0,1:T(8,128)(2,1)S(1)}, u32[]{:S(2)}, u32[]{:S(2)}) %all-to-all-start.3) | async-done | bytes 2097184 | tf_op jit(solution)/shard_map/all_to_all | solution.py:329
  143.5 142.2 %all-gather.6.cloned.1.call-done = bf16[64,16,4096]{2,1,0:T(8,128)(2,1)} async-done(((bf16[2,16,4096]{2,1,0:T(8,128)(2,1)}), bf16[64,16,4096]{2,1,0:T(8,128)(2,1)}) %all-gather.6.cloned.1.call-update) | async-done | bytes 8388624 | tf_op jit(solution)/shard_map/all_gather | solution.py:330
  285.8 5.7 %fusion.11 = bf16[256,2,32,16]{0,3,1,2:T(8,128)(2,1)S(1)} fusion(bf16[32,2,16,4096]{3,2,1,0:T(8,128)(2,1)} %bitcast.43, bf16[4096,256,1,1]{1,0,3,2:T(8,128)(2,1)S(1)} %bitcast.37), kind=kOutput, calls=%fused_computation.9 | convolution fusion | flops 2147745792 | bytes 11010048 | tf_op jit(solution)/shard_map/td,gkct->dkgc/dot_general | solution.py:331
  291.5 1.2 copy.32
  292.7 32.1 %reduce-scatter.2.cloned.1.call-done = bf16[128,2048]{1,0:T(8,128)(2,1)} async-done(((bf16[128,8192]{1,0:T(8,128)(2,1)}), bf16[128,2048]{1,0:T(8,128)(2,1)}) %reduce-scatter.2.cloned.1.call-update) | async-done | bytes 524304 | tf_op jit(solution)/shard_map/reduce_scatter | solution.py:326
  (4 shorter events, 0.1 us)
Async XLA Ops:
  7.2 50.6 %copy-start = (f32[2,3,512]{2,0,1:T(2,128)S(1)}, f32[2,3,512]{2,0,1:T(2,128)}, u32[]{:S(2)}) copy-start(f32[2,3,512]{2,0,1:T(2,128)} %param.9) | copy-start | bytes 36868
  7.2 31.6 %all-gather.4.cloned.1.call-start = ((), (), s32[]{:S(2)}) async-start(), calls=%async_computation.5 | async-start | bytes 2621440 | tf_op jit(solution)/shard_map/all_gather | solution.py:312
  7.9 42.5 %all-to-all-start.1 = ((bf16[32,16,128]{2,1,0:T(8,128)(2,1)}), bf16[32,16,128]{2,1,0:T(8,128)(2,1)S(1)}, u32[]{:S(2)}, u32[]{:S(2)}) async-start(bf16[32,16,128]{2,1,0:T(8,128)(2,1)} %bitcast.41), calls=%async_computation.1 | async-start | bytes 262144 | tf_op jit(solution)/shard_map/all_to_all | solution.py:313
  17.2 50.4 %copy-start.1 = (f32[16,4096]{1,0:T(8,128)S(1)}, f32[16,4096]{1,0:T(8,128)}, u32[]{:S(2)}) copy-start(f32[16,4096]{1,0:T(8,128)} %filt_ref.1) | copy-start | bytes 786436
  17.2 50.4 %copy-start.2 = (bf16[4,256,256]{2,1,0:T(8,128)(2,1)S(1)}, bf16[4,256,256]{2,1,0:T(8,128)(2,1)}, u32[]{:S(2)}) copy-start(bf16[4,256,256]{2,1,0:T(8,128)(2,1)} %constant.14.clone.mat_ref) | copy-start | bytes 1572868
  17.2 50.4 %copy-start.3 = (f32[4,33,128]{2,1,0:T(8,128)S(1)}, f32[4,33,128]{2,1,0:T(8,128)}, u32[]{:S(2)}) copy-start(f32[4,33,128]{2,1,0:T(8,128)} %constant.15.clone.turn_ref) | copy-start | bytes 202756
  50.5 17.1 %all-to-all-start = ((bf16[32,2,16,128]{3,2,1,0:T(8,128)(2,1)}), bf16[32,2,16,128]{3,2,1,0:T(8,128)(2,1)S(1)}, u32[]{:S(2)}, u32[]{:S(2)}) async-start(bf16[32,2,16,128]{3,2,1,0:T(8,128)(2,1)} %bitcast.35), calls=%async_computation | async-start | bytes 524288 | tf_op jit(solution)/shard_map/all_to_all | solution.py:318
  57.7 228.0 %all-gather.6.cloned.1.call-start = ((), (), s32[]{:S(2)}) async-start(), calls=%async_computation.7 | async-start | bytes 8650752 | tf_op jit(solution)/shard_map/all_gather | solution.py:330
  71.9 252.9 %reduce-scatter.2.cloned.1.call-start = ((), (), s32[]{:S(2)}) async-start(), calls=%async_computation.6 | async-start | bytes 2621440 | tf_op jit(solution)/shard_map/reduce_scatter | solution.py:326
  88.9 13.1 %copy-start.4 = (bf16[128,8192]{1,0:T(8,128)(2,1)S(1)}, bf16[128,8192]{1,0:T(8,128)(2,1)}, u32[]{:S(2)}) copy-start(bf16[128,8192]{1,0:T(8,128)(2,1)} %all-gather.4.cloned.1.call-done) | copy-start | bytes 6291460
  103.6 39.9 %all-to-all-start.3 = ((bf16[128,32,256]{2,0,1:T(8,128)(2,1)}), bf16[128,32,256]{2,0,1:T(8,128)(2,1)S(1)}, u32[]{:S(2)}, u32[]{:S(2)}) async-start(bf16[128,32,256]{2,0,1:T(8,128)(2,1)} %bitcast.34), calls=%async_computation.4 | async-start | bytes 4194304 | tf_op jit(solution)/shard_map/all_to_all | solution.py:329
Sparse Core Ops, SparseCore 0:
  9.7 29.0 all-gather.3
  72.0 213.6 all-gather.5
  289.0 35.7 reduce-scatter.1

commit v2 on v1

--- a/solution.py
+++ b/solution.py
@@ -91,13 +91,6 @@
         full = dft(line, -1)
         results += {0: full[:5], 4: full[:4]}.get(first, full)
     return results
-
-
-def real_sum(values, index):
-    total = None
-    for j, entry in enumerate(values):
-        total = add(total, turned(entry, j * index, 8)[0])
-    return total
 
 
 def real_line(values, count):
@@ -186,7 +179,7 @@
 
 def conv_kernel(
     proj_ref, cot_ref, filt_ref, taps_ref, mat_ref, turn_ref,
-    back_ref, pair_ref, fgrad_ref,
+    back_ref, fgrad_ref,
     gate_ref, value_ref, gfilt_ref, gval_ref, spec_ref, prod_ref,
 ):
     channels = filt_ref.shape[0]
@@ -274,7 +267,6 @@
                 total = total + taps_ref[stream, lead] * led(here, after, lead)
             total = total.astype(jnp.bfloat16)
             back_ref[n, stream] = total
-            pair_ref[stream, :, n * INNER : (n + 1) * INNER] = total
 
 
 def convolved(projected, cotangent, filters, taps):
@@ -285,11 +277,10 @@
         conv_kernel,
         out_shape=(
             jax.ShapeDtypeStruct((HALF, 3, channels, INNER), jnp.bfloat16),
-            jax.ShapeDtypeStruct((2, channels, length), jnp.bfloat16),
             jax.ShapeDtypeStruct((channels, length), jnp.float32),
         ),
         in_specs=[pl.BlockSpec(memory_space=pltpu.VMEM)] * 6,
-        out_specs=[pl.BlockSpec(memory_space=pltpu.VMEM)] * 3,
+        out_specs=[pl.BlockSpec(memory_space=pltpu.VMEM)] * 2,
         scratch_shapes=[
             f32((HALF, channels, INNER)),
             f32((HALF, channels, INNER)),
@@ -304,33 +295,606 @@
     )(projected, cotangent, filters, taps, jnp.asarray(matrices), jnp.asarray(turns))
 
 
+MESH = pl.DeviceIdType.MESH
+CHUNK = 512
+
+
+def coords():
+    dp = lax.axis_index("dp")
+    context = lax.axis_index("context")
+    return dp // 2, dp % 2, context // 8, (context // 2) % 4, context % 2
+
+
+def device(y_hi, core, z, x, y_lo):
+    return (y_hi * 2 + core, z * 8 + x * 2 + y_lo)
+
+
+def greet(partner):
+    pl.semaphore_signal(
+        pltpu.get_barrier_semaphore(), inc=1, device_id=partner, device_id_type=MESH
+    )
+
+
+def remote(src, dst, send_sem, recv_sem, partner):
+    return pltpu.make_async_remote_copy(
+        src_ref=src,
+        dst_ref=dst,
+        send_sem=send_sem,
+        recv_sem=recv_sem,
+        device_id=partner,
+        device_id_type=MESH,
+    )
+
+
+def greet_line():
+    dp = lax.axis_index("dp")
+    context = lax.axis_index("context")
+
+    @pl.loop(1, 32)
+    def _(i):
+        greet((dp, lax.rem(context + i, 32)))
+
+    @pl.loop(1, 4)
+    def _(i):
+        greet((lax.rem(dp + i, 4), context))
+
+
+def gather_kernel(
+    tok_ref, cot_ref, flat_ref,
+    wide_ref, proj_ref, cotg_ref, plane_ref,
+    stage, loose, wide, gathered, outgoing, total,
+    load_sem, store_sem, pair_send, pair_recv, half_send, half_recv, pass_send, pass_recv,
+    spread_send, spread_recv, swap_sem, proj_send, proj_recv, cot_send, cot_recv,
+):
+    y_hi, core, z, x, y_lo = coords()
+    dp = lax.axis_index("dp")
+    context = lax.axis_index("context")
+    rows, part = tok_ref.shape
+    sibling = device(y_hi, 1 - core, z, x, y_lo)
+    opposite = device(1 - y_hi, core, z, x, y_lo)
+    slot = z * 4 + x
+    chunks = part // CHUNK
+    flat_rows = CHUNK * 8
+
+    def quarter(j):
+        return 2 * lax.rem(y_hi + j // 2, 2) + lax.rem(core + j % 2, 2)
+
+    def chunk_of(step):
+        return quarter(step // chunks) * chunks + step % chunks
+
+    def load(step):
+        at = pl.ds(pl.multiple_of(chunk_of(step) * flat_rows, flat_rows), flat_rows)
+        return pltpu.make_async_copy(flat_ref.at[at], stage.at[step % 4], load_sem.at[step % 4])
+
+    def store(step):
+        at = pl.ds(pl.multiple_of(chunk_of(step) * CHUNK, CHUNK), CHUNK)
+        return pltpu.make_async_copy(wide.at[at], wide_ref.at[at], store_sem.at[step])
+
+    def separate(first, last):
+        @pl.loop(first, last)
+        def _(step):
+            load(step).wait()
+            loose[...] = stage[step % 4].astype(jnp.float32)
+            at = pl.ds(pl.multiple_of(chunk_of(step) * CHUNK, CHUNK), CHUNK)
+            for stream in range(2):
+                for tile in range(4):
+                    column = stream * 512 + tile * INNER
+                    wide[at, column : column + INNER] = loose[
+                        pl.ds(2 * tile + stream, CHUNK, stride=8), :
+                    ].astype(jnp.bfloat16)
+            store(step).start()
+
+            @pl.when(step + 4 < 4 * chunks)
+            def _():
+                load(step + 4).start()
+
+    def multiply(j, first, last):
+        for piece in range(first, last):
+            at = pl.ds(pl.multiple_of((quarter(j) * chunks + piece) * CHUNK, CHUNK), CHUNK)
+            total[...] += jnp.dot(
+                gathered[quarter(j), :, piece * CHUNK : (piece + 1) * CHUNK],
+                wide[at, :],
+                preferred_element_type=jnp.float32,
+            )
+
+    for step in range(4):
+        load(step).start()
+    greet_line()
+
+    @pl.loop(1, 16)
+    def _(i):
+        other = lax.rem(slot + i, 16)
+        greet(device(y_hi, 1 - core, other // 4, other % 4, y_lo))
+
+    pl.semaphore_wait(pltpu.get_barrier_semaphore(), 34 + 15)
+
+    half = part // 2
+    halves = [
+        remote(
+            tok_ref.at[:, i * half : (i + 1) * half],
+            gathered.at[dp, :, i * half : (i + 1) * half],
+            half_send.at[i], half_recv.at[i], opposite,
+        )
+        for i in range(2)
+    ]
+    to_sibling = remote(tok_ref, gathered.at[dp], pair_send.at[0], pair_recv.at[0], sibling)
+    halves[0].start()
+    to_sibling.start()
+    halves[1].start()
+
+    far = 2 * (1 - y_hi) + core
+
+    def spread(which, i, block):
+        to_x = lax.rem(x + i // 2, 4)
+        to_core = i % 2
+        column = pl.multiple_of(512 * to_x + 256 * to_core, 256)
+        src = gathered.at[block, :, pl.ds(column, 256)]
+        here = (block == z) & (to_x == x) & (to_core == core)
+        there = remote(
+            src, plane_ref.at[to_core, slot], spread_send.at[which * 8 + i], spread_recv.at[slot],
+            device(y_hi, to_core, block, to_x, y_lo),
+        )
+        return here, there, src
+
+    def spread_start(which, block):
+        @pl.loop(0, 8)
+        def _(i):
+            here, there, src = spread(which, i, block)
+
+            @pl.when(here)
+            def _():
+                pltpu.make_async_copy(src, plane_ref.at[core, slot], spread_recv.at[slot]).start()
+
+            @pl.when(jnp.logical_not(here))
+            def _():
+                there.start()
+
+    def spread_done(which, block):
+        @pl.loop(0, 8)
+        def _(i):
+            here, there, _src = spread(which, i, block)
+
+            @pl.when(jnp.logical_not(here))
+            def _():
+                there.wait_send()
+
+    gathered[dp] = tok_ref[...]
+    spread_start(0, dp)
+
+    def cot_copy(i):
+        to = lax.rem(context + i, 32)
+        return remote(cot_ref.at[to], cotg_ref.at[context], cot_send.at[i], cot_recv.at[i], (dp, to))
+
+    @pl.loop(1, 32)
+    def _(i):
+        cot_copy(i).start()
+
+    cotg_ref[context] = cot_ref[context]
+    total[...] = jnp.zeros_like(total)
+    separate(0, 4)
+    multiply(0, 0, 4)
+    separate(4, 8)
+    to_sibling.wait_recv()
+    multiply(1, 0, 4)
+    separate(8, 11)
+
+    passed = [
+        remote(
+            gathered.at[far, :, i * half : (i + 1) * half],
+            gathered.at[far, :, i * half : (i + 1) * half],
+            pass_send.at[i], pass_recv.at[i], sibling,
+        )
+        for i in range(2)
+    ]
+    halves[0].wait_recv()
+    passed[0].start()
+    separate(11, 14)
+    multiply(2, 0, 2)
+    halves[1].wait_recv()
+    passed[1].start()
+    spread_start(1, far)
+    separate(14, 16)
+    multiply(2, 2, 4)
+    passed[0].wait_recv()
+    multiply(3, 0, 2)
+    passed[1].wait_recv()
+    multiply(3, 2, 4)
+    outgoing[...] = total[...].T.astype(jnp.bfloat16).reshape(outgoing.shape)
+
+    def proj_copy(i):
+        to = lax.rem(context + i, 32)
+        return remote(
+            outgoing.at[:, to], proj_ref.at[context], proj_send.at[i], proj_recv.at[i], (dp, to)
+        )
+
+    @pl.loop(1, 32)
+    def _(i):
+        proj_copy(i).start()
+
+    proj_ref[context] = outgoing[:, context]
+
+    @pl.loop(0, 16)
+    def _(i):
+        remote(
+            plane_ref.at[core, i], plane_ref.at[core, i], spread_send.at[0], spread_recv.at[i], sibling
+        ).wait_recv()
+
+    swap = remote(plane_ref.at[core], plane_ref.at[core], swap_sem.at[0], swap_sem.at[1], sibling)
+    swap.start()
+
+    @pl.loop(1, 32)
+    def _(i):
+        proj_copy(i).wait()
+        cot_copy(i).wait()
+
+    @pl.loop(0, 16)
+    def _(step):
+        store(step).wait()
+
+    for copy in halves + [to_sibling] + passed:
+        copy.wait_send()
+    spread_done(0, dp)
+    spread_done(1, far)
+    swap.wait()
+
+
+def projected_groups(tokens, cotangent, flat):
+    rows, part = tokens.shape
+    depth, width = 4 * part, 1024
+    bf16 = functools.partial(jax.ShapeDtypeStruct, dtype=jnp.bfloat16)
+    dma = lambda n: pltpu.SemaphoreType.DMA((n,))
+    vmem = pl.BlockSpec(memory_space=pltpu.VMEM)
+    hbm = pl.BlockSpec(memory_space=pl.ANY)
+    return pl.pallas_call(
+        gather_kernel,
+        out_shape=(
+            bf16((depth, width)),
+            bf16((32, 2, 16, rows)),
+            bf16((32, 16, rows)),
+            bf16((2, 16, rows, 256)),
+        ),
+        in_specs=[vmem, vmem, hbm],
+        out_specs=[hbm, vmem, vmem, vmem],
+        scratch_shapes=[
+            pltpu.VMEM((4, CHUNK * 8, INNER), jnp.bfloat16),
+            pltpu.VMEM((CHUNK * 8, INNER), jnp.float32),
+            pltpu.VMEM((depth, width), jnp.bfloat16),
+            pltpu.VMEM((4, rows, part), jnp.bfloat16),
+            pltpu.VMEM((2, 32, 16, rows), jnp.bfloat16),
+            pltpu.VMEM((rows, width), jnp.float32),
+            dma(4), dma(16), dma(1), dma(1), dma(2), dma(2), dma(2), dma(2),
+            dma(16), dma(16), dma(2), dma(32), dma(32), dma(32), dma(32),
+        ],
+        compiler_params=pltpu.CompilerParams(
+            collective_id=0, has_side_effects=True, vmem_limit_bytes=50 * 1024 * 1024
+        ),
+        cost_estimate=pl.CostEstimate(
+            flops=2_200_000_000, bytes_accessed=36_000_000, transcendentals=0
+        ),
+        name="gather_and_project",
+    )(tokens, cotangent, flat)
+
+
+def gradient_kernel(
+    back_ref, plane_ref, wide_ref,
+    gated_ref, tgrad_ref, wgrad_ref,
+    wide, blocks, sums, leaving, arriving, far_out, far_in, own, swap_out, swap_in,
+    load_sem, proj_send, proj_recv, gated_send, gated_recv, sib_send, sib_recv, far_sem,
+    ring_send, ring_recv, swap_send, swap_recv,
+):
+    y_hi, core, z, x, y_lo = coords()
+    dp = lax.axis_index("dp")
+    context = lax.axis_index("context")
+    sibling = device(y_hi, 1 - core, z, x, y_lo)
+    opposite = device(1 - y_hi, core, z, x, y_lo)
+    slot = z * 4 + x
+    depth = wide.shape[0]
+    piece = depth // 16
+    quarter_rows = depth // 4
+
+    def load(i):
+        at = pl.ds(pl.multiple_of(i * piece, piece), piece)
+        return pltpu.make_async_copy(wide_ref.at[at], wide.at[at], load_sem.at[i])
+
+    @pl.loop(0, 16)
+    def _(i):
+        load(i).start()
+
+    greet_line()
+    pl.semaphore_wait(pltpu.get_barrier_semaphore(), 34)
+
+    def proj_copy(i):
+        to = lax.rem(context + i, 32)
+        to_slot = (to // 8) * 4 + (to // 2) % 4
+        return remote(
+            back_ref.at[to, pl.ds(0, 2)], blocks.at[to_slot, :, context],
+            proj_send.at[i], proj_recv.at[i], (dp, to),
+        )
+
+    def proj_arrival(i):
+        source = lax.rem(context + 32 - i, 32)
+        return remote(
+            back_ref.at[source, pl.ds(0, 2)], blocks.at[slot, :, source],
+            proj_send.at[i], proj_recv.at[i], (dp, source),
+        )
+
+    def gated_copy(i):
+        to = lax.rem(context + i, 32)
+        return remote(
+            back_ref.at[to, 2], gated_ref.at[context], gated_send.at[i], gated_recv.at[i], (dp, to)
+        )
+
+    @pl.loop(1, 32)
+    def _(i):
+        proj_copy(i).start()
+
+    @pl.loop(1, 32)
+    def _(i):
+        gated_copy(i).start()
+
+    blocks[slot, :, context] = back_ref[context, pl.ds(0, 2)]
+    gated_ref[context] = back_ref[context, 2]
+
+    @pl.loop(1, 32)
+    def _(i):
+        proj_arrival(i).wait_recv()
+
+    def place(first, along, across):
+        if first == "x":
+            return lax.rem(z + across + 4, 4) * 4 + lax.rem(x + along + 4, 4)
+        return lax.rem(z + along + 4, 4) * 4 + lax.rem(x + across + 4, 4)
+
+    def neighbour(first, along, across):
+        at = place(first, along, across)
+        return device(y_hi, core, at // 4, at % 4, y_lo)
+
+    class Unit:
+        def __init__(self, number):
+            self.stream = number // 2
+            self.part = number % 2
+            self.first = ("x", "z")[self.part]
+            self.base = 20 * number
+            self.started = []
+
+        def rows(self, at, part):
+            begin, count = {None: (0, 16), 0: (0, 8), 1: (8, 8)}[part]
+            return blocks.at[at, self.stream, pl.ds(16 * self.part + begin, count)]
+
+        def copy(self, index, along, across, part, step_along, step_across):
+            ref = self.rows(place(self.first, along, across), part)
+            return remote(
+                ref, ref, ring_send.at[self.base + index], ring_recv.at[self.base + index],
+                neighbour(self.first, step_along, step_across),
+            )
+
+        def send(self, *args):
+            copy = self.copy(*args)
+            copy.start()
+            self.started.append(copy)
+
+        def arrived(self, index, along, across, part):
+            self.copy(index, along, across, part, 1, 0).wait_recv()
+
+        def send_line(self, which, along):
+            self.send(4 + 4 * which, along, 0, None, 0, 1)
+            self.send(5 + 4 * which, along, 0, None, 0, -1)
+
+        def pass_line(self, which, along):
+            self.arrived(4 + 4 * which, along, -1, None)
+            self.send(6 + 4 * which, along, -1, 0, 0, 1)
+            self.arrived(5 + 4 * which, along, 1, None)
+            self.send(7 + 4 * which, along, 1, 1, 0, -1)
+
+        def end_line(self, which, along):
+            self.arrived(6 + 4 * which, along, -2, 0)
+            self.arrived(7 + 4 * which, along, 2, 1)
+
+        def begin(self):
+            self.send(0, 0, 0, None, 1, 0)
+            self.send(1, 0, 0, None, -1, 0)
+            self.send_line(0, 0)
+
+        def second(self):
+            self.arrived(0, -1, 0, None)
+            self.send(2, -1, 0, 0, 1, 0)
+            self.send_line(1, -1)
+            self.arrived(1, 1, 0, None)
+            self.send(3, 1, 0, 1, -1, 0)
+            self.send_line(2, 1)
+            self.pass_line(0, 0)
+
+        def third(self):
+            self.arrived(2, -2, 0, 0)
+            self.arrived(3, 2, 0, 1)
+            self.send_line(3, 2)
+            self.pass_line(1, -1)
+            self.pass_line(2, 1)
+
+        def fourth(self):
+            self.pass_line(3, 2)
+            self.end_line(0, 0)
+            self.end_line(1, -1)
+            self.end_line(2, 1)
+            self.end_line(3, 2)
+
+    units = [Unit(number) for number in range(4)]
+
+    def accumulate(stream):
+        sums[:, stream] = jnp.zeros(sums.shape[:1] + sums.shape[2:], jnp.float32)
+
+        @pl.loop(0, 16)
+        def _(at):
+            block = blocks[at, stream].reshape(512, INNER)
+            for half in range(2):
+                sums[half, stream] += jnp.dot(
+                    block, plane_ref[half, at], preferred_element_type=jnp.float32
+                )
+
+    def weight_copy(stream):
+        return remote(
+            swap_out.at[stream], swap_in.at[stream], swap_send.at[stream], swap_recv.at[stream],
+            device(y_hi, core, z, x, 1 - y_lo),
+        )
+
+    def weight_send(stream):
+        accumulate(stream)
+        swap_out[stream] = sums[1 - y_lo, stream].astype(jnp.bfloat16)
+        weight_copy(stream).start()
+
+    def weight_end(stream):
+        weight_copy(stream).wait_recv()
+        full = sums[y_lo, stream] + swap_in[stream].astype(jnp.float32)
+        wgrad_ref[:, stream * 512 : (stream + 1) * 512] = full.T.astype(jnp.bfloat16)
+
+    def product(q, put):
+        held = blocks[slot].reshape(1024, INNER)
+
+        @pl.loop(0, quarter_rows // CHUNK)
+        def _(i):
+            at = pl.ds(pl.multiple_of(q * quarter_rows + i * CHUNK, CHUNK), CHUNK)
+            put(
+                pl.ds(pl.multiple_of(i * CHUNK, CHUNK), CHUNK),
+                jnp.dot(wide[at, :], held, preferred_element_type=jnp.float32),
+            )
+
+    def to_sibling(which):
+        return remote(
+            leaving.at[which], arriving.at[which], sib_send.at[which], sib_recv.at[which], sibling
+        )
+
+    def for_sibling(which, y):
+        def put(at, value):
+            leaving[which, at, :] = value.astype(jnp.bfloat16)
+
+        product(2 * y + 1 - core, put)
+        to_sibling(which).start()
+
+    def keep(y):
+        def put(at, value):
+            own[at, :] = value
+
+        product(2 * y + core, put)
+
+    far_copy = remote(far_out, far_in, far_sem.at[0], far_sem.at[1], opposite)
+
+    units[0].begin()
+    units[1].begin()
+
+    @pl.loop(0, 16)
+    def _(i):
+        load(i).wait()
+
+    for_sibling(0, 1 - y_hi)
+    units[0].second()
+    units[1].second()
+    units[2].begin()
+    units[3].begin()
+    keep(1 - y_hi)
+    to_sibling(0).wait_recv()
+    far_out[...] = (own[...] + arriving[0].astype(jnp.float32)).astype(jnp.bfloat16)
+    far_copy.start()
+    units[0].third()
+    units[1].third()
+    units[2].second()
+    units[3].second()
+    for_sibling(1, y_hi)
+    units[0].fourth()
+    units[1].fourth()
+    units[2].third()
+    units[3].third()
+    weight_send(0)
+    keep(y_hi)
+    to_sibling(1).wait_recv()
+    own[...] += arriving[1].astype(jnp.float32)
+    far_copy.wait_recv()
+    for i in range(4):
+        at = pl.ds(i * CHUNK, CHUNK)
+        tgrad_ref[:, i * CHUNK : (i + 1) * CHUNK] = (
+            (own[at, :] + far_in[at, :].astype(jnp.float32)).T.astype(jnp.bfloat16)
+        )
+    units[2].fourth()
+    units[3].fourth()
+    weight_send(1)
+    weight_end(0)
+    weight_end(1)
+
+    @pl.loop(1, 32)
+    def _(i):
+        proj_copy(i).wait_send()
+        gated_copy(i).wait()
+
+    for unit in units:
+        for copy in unit.started:
+            copy.wait_send()
+    far_copy.wait_send()
+    for i in range(2):
+        to_sibling(i).wait_send()
+        weight_copy(i).wait_send()
+
+
+def gradients(back, plane, wide):
+    depth = wide.shape[0]
+    bf16 = functools.partial(jax.ShapeDtypeStruct, dtype=jnp.bfloat16)
+    dma = lambda n: pltpu.SemaphoreType.DMA((n,))
+    vmem = pl.BlockSpec(memory_space=pltpu.VMEM)
+    hbm = pl.BlockSpec(memory_space=pl.ANY)
+    return pl.pallas_call(
+        gradient_kernel,
+        out_shape=(
+            bf16((32, 16, INNER)),
+            bf16((INNER, depth // 4)),
+            bf16((256, 1024)),
+        ),
+        in_specs=[vmem, vmem, hbm],
+        out_specs=[vmem, vmem, vmem],
+        scratch_shapes=[
+            pltpu.VMEM((depth, 1024), jnp.bfloat16),
+            pltpu.VMEM((16, 2, 32, 16, INNER), jnp.bfloat16),
+            pltpu.VMEM((2, 2, 512, 256), jnp.float32),
+            pltpu.VMEM((2, depth // 4, INNER), jnp.bfloat16),
+            pltpu.VMEM((2, depth // 4, INNER), jnp.bfloat16),
+            pltpu.VMEM((depth // 4, INNER), jnp.bfloat16),
+            pltpu.VMEM((depth // 4, INNER), jnp.bfloat16),
+            pltpu.VMEM((depth // 4, INNER), jnp.float32),
+            pltpu.VMEM((2, 512, 256), jnp.bfloat16),
+            pltpu.VMEM((2, 512, 256), jnp.bfloat16),
+            dma(16), dma(32), dma(32), dma(32), dma(32), dma(2), dma(2), dma(2),
+            dma(80), dma(80), dma(2), dma(2),
+        ],
+        compiler_params=pltpu.CompilerParams(
+            collective_id=1, has_side_effects=True, vmem_limit_bytes=50 * 1024 * 1024
+        ),
+        cost_estimate=pl.CostEstimate(
+            flops=4_400_000_000, bytes_accessed=36_000_000, transcendentals=0
+        ),
+        name="gradients",
+    )(back, plane, wide)
+
+
 def on_device(tokens, in_weight, short_taps, filters, cotangent):
     channels, length = filters.shape
     groups = lax.axis_size("context")
     rows = tokens.shape[0]
-    slab = in_weight.shape[2]
-    gathered = lax.all_gather(tokens, "dp", axis=1, tiled=True)
-    cot_group = lax.all_to_all(
-        cotangent.reshape(groups, channels, rows), "context", split_axis=0, concat_axis=0, tiled=True
+    depth, streams, slab = in_weight.shape
+    tiles = slab // INNER
+    flat = (
+        in_weight.reshape(depth, streams, tiles, INNER)
+        .transpose(0, 2, 1, 3)
+        .reshape(depth * streams * tiles, INNER)
     )
-    projected = jnp.einsum("td,dkc->kct", gathered, in_weight, preferred_element_type=jnp.float32)
-    outgoing = projected.astype(jnp.bfloat16).reshape(2, groups, channels, rows).transpose(1, 0, 2, 3)
-    proj_group = lax.all_to_all(outgoing, "context", split_axis=0, concat_axis=0, tiled=True)
+    wide, proj_group, cot_group, plane = projected_groups(
+        tokens, cotangent.reshape(groups, channels, rows), flat
+    )
     own = lax.dynamic_slice_in_dim(short_taps, lax.axis_index("context") * channels, channels, axis=2)
     taps = jnp.broadcast_to(own[..., None], own.shape + (INNER,))
-    back, pair, filter_grad = convolved(proj_group, cot_group, filters, taps)
-    back = lax.all_to_all(back, "context", split_axis=0, concat_axis=0, tiled=True)
-    gated_out = back[:, 2].reshape(slab, rows)
-    proj_grad = back[:, :2].transpose(1, 0, 2, 3).reshape(2, slab, rows)
-    partial_value = jnp.einsum("kct,dkc->td", proj_grad, in_weight, preferred_element_type=jnp.float32)
-    token_grad = lax.psum_scatter(
-        partial_value.astype(jnp.bfloat16), "dp", scatter_dimension=1, tiled=True
+    back, filter_grad = convolved(proj_group, cot_group, filters, taps)
+    gated_out, token_grad, weight_grad = gradients(back, plane, wide)
+    return (
+        gated_out.reshape(slab, rows),
+        token_grad,
+        weight_grad.reshape(weight_grad.shape[0], streams, slab),
+        filter_grad,
     )
-    tokens_own = lax.all_to_all(gathered, "context", split_axis=1, concat_axis=0, tiled=True)
-    whole = lax.all_gather(pair, "context", axis=0, tiled=False)
-    weight_grad = jnp.einsum("td,gkct->dkgc", tokens_own, whole, preferred_element_type=jnp.float32)
-    weight_grad = weight_grad.astype(jnp.bfloat16).reshape(tokens_own.shape[1], 2, slab)
-    return (gated_out, token_grad, weight_grad, filter_grad)
 
 
 def solution(mesh):

time: 332 us -> 116 us (0.35)
  waiting for transfers between devices: 241 us -> 0 us
  Pallas kernels: 4.26 us -> 110 us
  matrix products: 29.7 us -> 0 us
  starting transfers between devices: 20.8 us -> 0 us
  blocking collectives: 16.9 us -> 0 us
  between operations: 13.9 us -> 0.7 us
    all_gather x2 -> x0, waiting for transfers between devices: 164 us -> none  [the longest x1 142 us: on_device(): whole = lax.all_gather(pair, 'context', axis=0, tiled=False)]
    pallas_call x0 -> x2, Pallas kernels: none -> 106 us  [the longest x1 66 us: gradients(): pl.pallas_call(gradient_kernel, out_shape=(bf16((32, 16, INNER)), bf16((I...]
    all_to_all x3 -> x0, waiting for transfers between devices: 44.8 us -> none  [the longest x1 35.1 us: on_device(): lax.all_to_all(gathered, 'context', split_axis=1, concat_axis=0, tiled=True)]
    reduce_scatter x1 -> x0, waiting for transfers between devices: 32.1 us -> none  [on_device(): lax.psum_scatter(partial_value.astype(jnp.bfloat16), 'dp', scatter_dimens...]
    dot_general x3 -> x0, matrix products: 29.7 us -> none  [the longest x1 13.1 us: on_device(): jnp.einsum('kct,dkc->td', proj_grad, in_weight, preferred_element_type=jn...]
    all_to_all x3 -> x0, starting transfers between devices: 20.7 us -> none  [the longest x1 9.27 us: on_device(): lax.all_to_all(cotangent.reshape(groups, channels, rows), 'context', spli...]
    all_to_all x1 -> x0, blocking collectives: 16.9 us -> none  [on_device(): lax.all_to_all(back, 'context', split_axis=0, concat_axis=0, tiled=True)]
  transfers between devices with their start and end apart: 6 -> 0, of which waited for: 5 -> 0; matrix products, arithmetic and copies ran while one was open for 10% -> 0% of each run, Pallas kernels for 0% -> 0%
where the time goes in v2:
time: 116 us
  Pallas kernels  110 us (95%)
  local copies, waits for them, and re-layouts  5.42 us (5%)
    pallas_call x1, Pallas kernels, gradients(): pl.pallas_call(gradient_kernel, out_shape=(bf16((32, 16, INNER)), bf16((I...  66 us
    pallas_call x1, Pallas kernels, projected_groups(): pl.pallas_call(gather_kernel, out_shape=(bf16((depth, width)), bf16((32,...  39.9 us
    unnamed x14, local copies, waits for them, and re-layouts  4.1 us
    pallas_call x1, Pallas kernels, convolved(): pl.pallas_call(conv_kernel, out_shape=(jax.ShapeDtypeStruct((HALF, 3, cha...  4.08 us

profile of v2, /device:TPU:0, one launch (start us, length us, event | category | flops | bytes accessed | tf_op | source)
XLA Modules:
  0.0 116.1 jit_solution(8585534318463145363)
XLA Ops:
  0.6 0.0 copy-start
  0.6 0.0 copy-start.5
  0.7 0.7 copy-done
  1.3 0.1 constant_dynamic-slice_fusion
  1.4 0.1 broadcast_in_dim.2.taps_ref
  1.5 0.0 copy-start.1
  1.5 1.0 copy-done.1
  2.5 0.0 copy-start.2
  2.6 0.9 copy-done.2
  3.5 0.0 copy-start.3
  3.5 0.0 copy-start.4
  3.5 39.9 %gather_and_project.1 = (bf16[8192,1024]{1,0:T(8,128)(2,1)}, bf16[32,2,16,128]{3,2,1,0:T(8,128)(2,1)S(1)}, bf16[32,16,128]{2,1,0:T(8,128)(2,1)S(1)}, bf16[2,16,128,256]{3,2,1,0:T(8,128)(2,1)S(1)}) custom-call(bf16[128,2048]{1,0:T(8,128)(2,1)S(1)} %copy-done.1, bf16[32,16,128]{2,1,0:T(8,128)(2,1)S(1)} %bitcast.7, bf16[65536,128]{1,0:T(8,128)(2,1)} %bitcast.9), custom_call_target="tpu_custom_call" | custom-call | flops 2200000000 | bytes 36000000 | tf_op jit(solution)/shard_map/gather_and_project/pallas_call | solution.py:548
  43.4 0.0 copy-done.5
  43.4 0.0 copy-done.3
  43.4 0.0 copy-done.4
  43.4 4.1 %long_convolutions.1 = (bf16[32,3,16,128]{3,2,1,0:T(8,128)(2,1)S(1)}, f32[16,4096]{1,0:T(8,128)}) custom-call(bf16[32,2,16,128]{3,2,1,0:T(8,128)(2,1)S(1)} %get-tuple-element.13.proj_ref, bf16[32,16,128]{2,1,0:T(8,128)(2,1)S(1)} %get-tuple-element.14.cot_ref, f32[16,4096]{1,0:T(8,128)S(1)} %copy-done.3, f32[2,3,16,128]{3,2,1,0:T(8,128)S(1)} %broadcast_in_dim.2.taps_ref, ...), custom_call_target="tpu_custom_call" | custom-call | flops 1300000000 | bytes 2000000 | tf_op jit(solution)/shard_map/long_convolutions/pallas_call | solution.py:276
  47.5 66.0 %gradients.1 = (bf16[32,16,128]{2,1,0:T(8,128)(2,1)S(1)}, bf16[128,2048]{1,0:T(8,128)(2,1)S(1)}, bf16[256,1024]{1,0:T(8,128)(2,1)S(1)}) custom-call(bf16[32,3,16,128]{3,2,1,0:T(8,128)(2,1)S(1)} %get-tuple-element.15.back_ref, bf16[2,16,128,256]{3,2,1,0:T(8,128)(2,1)S(1)} %get-tuple-element.16.plane_ref, bf16[8192,1024]{1,0:T(8,128)(2,1)} %get-tuple-element.17.wide_ref), custom_call_target="tpu_custom_call" | custom-call | flops 4400000000 | bytes 36000000 | tf_op jit(solution)/shard_map/gradients/pallas_call | solution.py:841
  113.5 1.2 %reshape.28 = bf16[256,2,512]{2,1,0:T(2,128)(2,1)} reshape(bf16[256,1024]{1,0:T(8,128)(2,1)S(1)} %get-tuple-element.20) | data formatting | bytes 1048576 | tf_op jit(solution)/shard_map/reshape | solution.py:895
  114.7 0.7 copy.15
  115.3 0.8 copy.16
  (1 shorter events, 0.0 us)
Async XLA Ops:
  0.6 0.7 copy-start
  0.6 42.7 %copy-start.5 = (f32[4,33,128]{2,1,0:T(8,128)S(1)}, f32[4,33,128]{2,1,0:T(8,128)}, u32[]{:S(2)}) copy-start(f32[4,33,128]{2,1,0:T(8,128)} %constant.15.clone.turn_ref) | copy-start | bytes 202756
  1.5 1.1 copy-start.1
  2.5 0.9 copy-start.2
  3.5 39.9 %copy-start.3 = (f32[16,4096]{1,0:T(8,128)S(1)}, f32[16,4096]{1,0:T(8,128)}, u32[]{:S(2)}) copy-start(f32[16,4096]{1,0:T(8,128)} %filt_ref.1) | copy-start | bytes 786436
  3.5 39.9 %copy-start.4 = (bf16[4,256,256]{2,1,0:T(8,128)(2,1)S(1)}, bf16[4,256,256]{2,1,0:T(8,128)(2,1)}, u32[]{:S(2)}) copy-start(bf16[4,256,256]{2,1,0:T(8,128)(2,1)} %constant.14.clone.mat_ref) | copy-start | bytes 1572868

commit v3 on v2

v3 whole, which is shorter than its diff:
```python
import functools
import math

import jax
import jax.numpy as jnp
import numpy as np
from jax import lax
from jax.experimental import pallas as pl
from jax.experimental.pallas import tpu as pltpu
from jax.sharding import PartitionSpec as P

OUTER = 64
INNER = 128
TOTAL = OUTER * INNER
HALF = OUTER // 2
KEPT = [0, 8, 16, 24, 32] + [k1 + 8 * k2 for k1 in (1, 2, 3) for k2 in range(8)] + [4, 12, 20, 28]
ROWS = len(KEPT)


def add(a, b):
    return b if a is None else a if b is None else a + b


def neg(a):
    return None if a is None else -a


def sub(a, b):
    return a if b is None else neg(b) if a is None else a - b


def scaled(a, factor):
    if a is None or abs(factor) < 1e-12:
        return None
    if abs(factor - 1) < 1e-12:
        return a
    if abs(factor + 1) < 1e-12:
        return -a
    return a * np.float32(factor)


def cadd(a, b):
    return (add(a[0], b[0]), add(a[1], b[1]))


def csub(a, b):
    return (sub(a[0], b[0]), sub(a[1], b[1]))


def turned(a, step, count):
    step %= count
    if (8 * step) % count == 0 and (8 * step // count) % 2 == 1:
        eighth = 8 * step // count
        root = math.sqrt(0.5)
        re, im = a
        if eighth == 1:
            pair = (sub(re, im), add(re, im))
        elif eighth == 3:
            pair = (neg(add(re, im)), sub(re, im))
        elif eighth == 5:
            pair = (sub(im, re), neg(add(re, im)))
        else:
            pair = (add(re, im), sub(im, re))
        return (scaled(pair[0], root), scaled(pair[1], root))
    angle = 2 * math.pi * step / count
    cos, sin = math.cos(angle), math.sin(angle)
    return (
        sub(scaled(a[0], cos), scaled(a[1], sin)),
        add(scaled(a[0], sin), scaled(a[1], cos)),
    )


def dft(values, sign):
    count = len(values)
    if count == 1:
        return values
    even = dft(values[0::2], sign)
    odd = dft(values[1::2], sign)
    odd = [turned(entry, sign * index, count) for index, entry in enumerate(odd)]
    return [cadd(a, b) for a, b in zip(even, odd)] + [csub(a, b) for a, b in zip(even, odd)]


def outer_forward(load):
    parts = []
    for second in range(8):
        line = [(load(8 * first + second), None) if first < 4 else (None, None) for first in range(8)]
        parts.append(dft(line, -1)[:5])
    results = []
    for first in (0, 1, 2, 3, 4):
        line = [turned(parts[second][first], -second * first, OUTER) for second in range(8)]
        full = dft(line, -1)
        results += {0: full[:5], 4: full[:4]}.get(first, full)
    return results


def real_line(values, count):
    top = values[0][0]
    last = values[4][0]
    a = add(top, last)
    b = sub(top, last)
    (r1, i1), (r2, i2), (r3, i3) = values[1:4]
    s13, d13 = add(r1, r3), sub(r1, r3)
    si, di = add(i1, i3), sub(i1, i3)
    root = math.sqrt(0.5)
    p = scaled(sub(d13, si), root)
    q = scaled(add(d13, si), root)
    out = [
        add(add(a, r2), s13),
        add(sub(b, i2), p),
        sub(sub(a, r2), di),
        sub(add(b, i2), q),
    ]
    if count > 4:
        out += [
            sub(add(a, r2), s13),
            sub(sub(b, i2), p),
            add(sub(a, r2), di),
            add(add(b, i2), q),
        ]
    return out


def outer_inverse(load):
    zero = real_line([load(row) for row in range(5)], 8)
    lines = []
    for first in (1, 2, 3):
        line = dft([load(5 + 8 * (first - 1) + second) for second in range(8)], 1)
        lines.append([turned(line[second], second * first, OUTER) for second in range(8)])
    tail = dft([load(29 + second) if second < 4 else (None, None) for second in range(8)], 1)
    tail = [turned(tail[second], second, 16)[0] for second in range(8)]
    results = [None] * HALF
    for second in range(8):
        line = [(zero[second], None)] + [lines[first][second] for first in range(3)] + [(tail[second], None)]
        for first, entry in enumerate(real_line(line, 4)):
            results[8 * first + second] = entry
    return results


def tables():
    index = np.arange(INNER, dtype=np.float64)
    angle = 2 * np.pi / INNER * (np.outer(index, index) % INNER)
    cos, sin = np.cos(angle), np.sin(angle)
    wide = np.block([[cos, -sin], [sin, cos]])
    high = wide.astype(jnp.bfloat16)
    low = (wide - high.astype(np.float64)).astype(jnp.bfloat16)
    inverse = wide.T
    inverse_high = inverse.astype(jnp.bfloat16)
    inverse_low = (inverse - inverse_high.astype(np.float64)).astype(jnp.bfloat16)
    matrices = np.stack([high, low, inverse_high, inverse_low])
    turn = 2 * np.pi / TOTAL * np.outer(np.array(KEPT, np.float64), index)
    weight = np.array([1.0 if k in (0, HALF) else 2.0 for k in KEPT])[:, None] / TOTAL
    turns = np.stack([np.cos(turn), np.sin(turn), weight * np.cos(turn), weight * np.sin(turn)])
    return matrices, turns.astype(np.float32)


def times_matrix(wide, high, low):
    top = wide.astype(jnp.bfloat16)
    rest = (wide - top.astype(jnp.float32)).astype(jnp.bfloat16)
    dot = functools.partial(jnp.dot, preferred_element_type=jnp.float32)
    return dot(top, high) + (dot(rest, high) + dot(top, low))


def lagged(here, before, lag):
    lane = lax.broadcasted_iota(jnp.int32, here.shape, here.ndim - 1)
    rolled = pltpu.roll(here, lag, here.ndim - 1)
    if before is None:
        return jnp.where(lane < lag, 0.0, rolled)
    return jnp.where(lane < lag, pltpu.roll(before, lag, here.ndim - 1), rolled)


def led(here, after, lead):
    lane = lax.broadcasted_iota(jnp.int32, here.shape, here.ndim - 1)
    width = here.shape[-1]
    rolled = pltpu.roll(here, width - lead, here.ndim - 1)
    if after is None:
        return jnp.where(lane >= width - lead, 0.0, rolled)
    return jnp.where(lane >= width - lead, pltpu.roll(after, width - lead, here.ndim - 1), rolled)


MESH = pl.DeviceIdType.MESH
CHUNK = 512
PIECES = 4


def coords():
    dp = lax.axis_index("dp")
    context = lax.axis_index("context")
    return dp // 2, dp % 2, context // 8, (context // 2) % 4, context % 2


def device(y_hi, core, z, x, y_lo):
    return (y_hi * 2 + core, z * 8 + x * 2 + y_lo)


def greet(partner):
    pl.semaphore_signal(
        pltpu.get_barrier_semaphore(), inc=1, device_id=partner, device_id_type=MESH
    )


def remote(src, dst, send_sem, recv_sem, partner):
    return pltpu.make_async_remote_copy(
        src_ref=src,
        dst_ref=dst,
        send_sem=send_sem,
        recv_sem=recv_sem,
        device_id=partner,
        device_id_type=MESH,
    )


def greet_line():
    dp = lax.axis_index("dp")
    context = lax.axis_index("context")

    @pl.loop(1, 32)
    def _(i):
        greet((dp, lax.rem(context + i, 32)))

    @pl.loop(1, 4)
    def _(i):
        greet((lax.rem(dp + i, 4), context))


def block_kernel(
    tok_ref, cot_ref, filt_ref, taps_ref, mat_ref, turn_ref, flat_ref,
    gated_ref, tgrad_ref, wgrad_ref, fgrad_ref,
    stage, loose, wide, gathered, outgoing, total, plane, proj, cot,
    fields, spec, prod, gate_ref, back,
    blocks, sums, leaving, arriving, far_out, far_in, own, swap_out, swap_in,
    load_sem, in_sem, pair_sem, half_send, half_recv, pass_send, pass_recv,
    spread_send, spread_recv, plane_sem, proj_send, proj_recv, cot_send, cot_recv,
    back_send, back_recv, gated_send, gated_recv, sib_send, sib_recv, far_sem,
    ring_send, ring_recv, swap_send, swap_recv,
):
    y_hi, core, z, x, y_lo = coords()
    dp = lax.axis_index("dp")
    context = lax.axis_index("context")
    rows, part = tok_ref.shape
    channels = filt_ref.shape[0]
    sibling = device(y_hi, 1 - core, z, x, y_lo)
    opposite = device(1 - y_hi, core, z, x, y_lo)
    slot = z * 4 + x
    lanes = pl.ds(pl.multiple_of(slot * INNER, INNER), INNER)
    chunks = part // CHUNK
    flat_rows = CHUNK * 8

    def quarter(j):
        return 2 * lax.rem(y_hi + j // 2, 2) + lax.rem(core + j % 2, 2)

    def chunk_of(step):
        return quarter(step // chunks) * chunks + step % chunks

    def load(step):
        at = pl.ds(pl.multiple_of(chunk_of(step) * flat_rows, flat_rows), flat_rows)
        return pltpu.make_async_copy(flat_ref.at[at], stage.at[step % 4], load_sem.at[step % 4])

    def separate(first, last):
        @pl.loop(first, last)
        def _(step):
            load(step).wait()
            loose[...] = stage[step % 4].astype(jnp.float32)
            at = pl.ds(pl.multiple_of(chunk_of(step) * CHUNK, CHUNK), CHUNK)
            for stream in range(2):
                for tile in range(4):
                    column = stream * 512 + tile * INNER
                    wide[at, column : column + INNER] = loose[
                        pl.ds(2 * tile + stream, CHUNK, stride=8), :
                    ].astype(jnp.bfloat16)

            @pl.when(step + 4 < 4 * chunks)
            def _():
                load(step + 4).start()

    def multiply(j, first, last):
        for piece in range(first, last):
            at = pl.ds(pl.multiple_of((quarter(j) * chunks + piece) * CHUNK, CHUNK), CHUNK)
            total[...] += jnp.dot(
                gathered[quarter(j), :, piece * CHUNK : (piece + 1) * CHUNK],
                wide[at, :],
                preferred_element_type=jnp.float32,
            )

    own_tokens = pltpu.make_async_copy(tok_ref, gathered.at[dp], in_sem.at[0])
    own_cot = pltpu.make_async_copy(cot_ref.at[context], cot.at[context], in_sem.at[1])
    own_tokens.start()
    own_cot.start()
    for step in range(4):
        load(step).start()
    greet_line()

    @pl.loop(1, 16)
    def _(i):
        other = lax.rem(slot + i, 16)
        greet(device(y_hi, 1 - core, other // 4, other % 4, y_lo))

    pl.semaphore_wait(pltpu.get_barrier_semaphore(), 34 + 15)

    width = part // PIECES
    pieces = [
        remote(
            tok_ref.at[:, i * width : (i + 1) * width],
            gathered.at[dp, :, i * width : (i + 1) * width],
            half_send.at[i], half_recv.at[i], opposite,
        )
        for i in range(PIECES)
    ]
    token_pair = remote(tok_ref, gathered.at[dp], pair_sem.at[0], pair_sem.at[1], sibling)
    pieces[0].start()
    token_pair.start()
    for copy in pieces[1:]:
        copy.start()
    own_tokens.wait()
    far = 2 * (1 - y_hi) + core
    passed = [
        remote(
            gathered.at[far, :, i * width : (i + 1) * width],
            gathered.at[far, :, i * width : (i + 1) * width],
            pass_send.at[i], pass_recv.at[i], sibling,
        )
        for i in range(PIECES)
    ]

    def spread(which, i, block):
        to_x = i // 2
        to_core = i % 2
        column = pl.multiple_of(512 * to_x + 256 * to_core, 256)
        src = gathered.at[block, :, pl.ds(column, 256)]
        here = (block == z) & (to_x == x) & (to_core == core)
        there = remote(
            src, plane.at[to_core, slot], spread_send.at[which * 8 + i], spread_recv.at[slot],
            device(y_hi, to_core, block, to_x, y_lo),
        )
        return here, there, src

    def spread_start(which, block, first, last):
        @pl.loop(first, last)
        def _(i):
            here, there, src = spread(which, i, block)

            @pl.when(here)
            def _():
                pltpu.make_async_copy(src, plane.at[core, slot], spread_recv.at[slot]).start()

            @pl.when(jnp.logical_not(here))
            def _():
                there.start()

    def spread_done(which, block):
        @pl.loop(0, 8)
        def _(i):
            here, there, _src = spread(which, i, block)

            @pl.when(jnp.logical_not(here))
            def _():
                there.wait_send()

    plane_copy = remote(plane.at[core], plane.at[core], plane_sem.at[0], plane_sem.at[1], sibling)

    spread_start(0, dp, 0, 8)

    def cot_copy(i):
        to = lax.rem(context + i, 32)
        return remote(cot_ref.at[to], cot.at[context], cot_send.at[i], cot_recv.at[i], (dp, to))

    @pl.loop(1, 32)
    def _(i):
        cot_copy(i).start()

    total[...] = jnp.zeros_like(total)
    separate(0, 4)
    multiply(0, 0, 4)
    separate(4, 7)
    token_pair.wait_recv()
    for n in range(HALF):
        fields[0, n] = filt_ref[:, n * INNER : (n + 1) * INNER]
    for i in range(PIECES):
        separate(7 + (9 * i) // PIECES, 7 + (9 * (i + 1)) // PIECES)
        if i == PIECES - 1:
            multiply(1, 0, 4)
            multiply(2, 0, 3)
        pieces[i].wait_recv()
        passed[i].start()
        if i % 2 == 1 and PIECES == 4:
            spread_start(1, far, 2 * i - 2, 2 * i + 2)
    multiply(2, 3, 4)
    for i in range(PIECES):
        passed[i].wait_recv()
        multiply(3, i, i + 1)
    outgoing[...] = total[...].T.astype(jnp.bfloat16).reshape(outgoing.shape)

    def proj_copy(i):
        to = lax.rem(context + i, 32)
        return remote(outgoing.at[:, to], proj.at[context], proj_send.at[i], proj_recv.at[i], (dp, to))

    @pl.loop(1, 32)
    def _(i):
        proj_copy(i).start()

    proj[context] = outgoing[:, context]

    @pl.loop(1, 32)
    def _(i):
        cot_copy(i).wait()

    own_cot.wait()

    @pl.loop(1, 32)
    def _(i):
        proj_copy(i).wait_recv()

    def short(stream, n):
        here = proj[n, stream].astype(jnp.float32)
        before = proj[n - 1, stream].astype(jnp.float32) if n else None
        result = taps_ref[stream, 0] * here
        for lag in (1, 2):
            result = result + taps_ref[stream, lag] * lagged(here, before, lag)
        return result

    for n in range(HALF):
        gate = short(0, n)
        gate_ref[n] = gate
        fields[2, n] = cot[n].astype(jnp.float32) * gate
        fields[1, n] = short(1, n)

    size = ROWS * channels

    @pl.loop(0, 3)
    def _(which):
        for row, (re, im) in enumerate(outer_forward(lambda n: fields[which, n])):
            cos = turn_ref[0, row][None, :]
            sin = turn_ref[1, row][None, :]
            at = pl.ds(row * channels, channels)
            if im is None:
                spec[which, at, :INNER] = re * cos
                spec[which, at, INNER:] = -(re * sin)
            else:
                spec[which, at, :INNER] = re * cos + im * sin
                spec[which, at, INNER:] = im * cos - re * sin
        spec[which] = times_matrix(spec[which], mat_ref[0], mat_ref[1])

    @pl.loop(0, ROWS)
    def _(row):
        at = pl.ds(pl.multiple_of(row * channels, channels), channels)
        (hr, hi), (vr, vi), (gr, gi) = [
            (spec[which, at, :INNER], spec[which, at, INNER:]) for which in range(3)
        ]

        def put(which, re, im):
            prod[which, at, :INNER] = re
            prod[which, at, INNER:] = im

        put(0, hr * vr - hi * vi, hr * vi + hi * vr)
        put(1, hr * gr + hi * gi, hr * gi - hi * gr)
        put(2, vr * gr + vi * gi, vr * gi - vi * gr)

    @pl.loop(0, 3)
    def _(which):
        prod[which] = times_matrix(prod[which], mat_ref[2], mat_ref[3])

        def turned_row(row):
            cos = turn_ref[2, row][None, :]
            sin = turn_ref[3, row][None, :]
            at = pl.ds(row * channels, channels)
            re, im = prod[which, at, :INNER], prod[which, at, INNER:]
            return re * cos - im * sin, im * cos + re * sin

        for n, entry in enumerate(outer_inverse(turned_row)):
            fields[which, n] = entry

    for n in range(HALF):
        entry = fields[0, n]
        back[n, 2] = (gate_ref[n] * entry).astype(back.dtype)
        gate_ref[n] = cot[n].astype(jnp.float32) * entry

    for stream, load_row in enumerate((lambda n: gate_ref[n], lambda n: fields[1, n])):
        for n in range(HALF):
            here = load_row(n)
            after = load_row(n + 1) if n + 1 < HALF else None
            result = taps_ref[stream, 0] * here
            for lead in (1, 2):
                result = result + taps_ref[stream, lead] * led(here, after, lead)
            back[n, stream] = result.astype(jnp.bfloat16)

    def group_rows(group):
        return pl.ds(pl.multiple_of(group * channels, channels), channels)

    def back_copy(i):
        to = lax.rem(context + i, 32)
        to_slot = (to // 8) * 4 + (to // 2) % 4
        to_lanes = pl.ds(pl.multiple_of(to_slot * INNER, INNER), INNER)
        return remote(
            back.at[to, pl.ds(0, 2)], blocks.at[:, group_rows(context), to_lanes],
            back_send.at[i], back_recv.at[i], (dp, to),
        )

    def back_arrival(i):
        source = lax.rem(context + 32 - i, 32)
        return remote(
            back.at[source, pl.ds(0, 2)], blocks.at[:, group_rows(source), lanes],
            back_send.at[i], back_recv.at[i], (dp, source),
        )

    def gated_copy(i):
        to = lax.rem(context + i, 32)
        return remote(
            back.at[to, 2], gated_ref.at[context], gated_send.at[i], gated_recv.at[i], (dp, to)
        )

    @pl.loop(1, 32)
    def _(i):
        back_copy(i).start()

    blocks[:, group_rows(context), lanes] = back[context, pl.ds(0, 2)]

    @pl.loop(1, 32)
    def _(i):
        gated_copy(i).start()

    gated_ref[context] = back[context, 2]
    for n in range(HALF):
        fgrad_ref[:, n * INNER : (n + 1) * INNER] = fields[2, n]

    @pl.loop(0, 16)
    def _(i):
        remote(
            plane.at[core, i], plane.at[core, i], spread_send.at[0], spread_recv.at[i], sibling
        ).wait_recv()

    plane_copy.start()

    @pl.loop(1, 32)
    def _(i):
        back_arrival(i).wait_recv()

    def place(first, along, across):
        if first == "x":
            return lax.rem(z + across + 4, 4) * 4 + lax.rem(x + along + 4, 4)
        return lax.rem(z + along + 4, 4) * 4 + lax.rem(x + across + 4, 4)

    def neighbour(first, along, across):
        at = place(first, along, across)
        return device(y_hi, core, at // 4, at % 4, y_lo)

    class Unit:
        def __init__(self, number):
            self.stream = number // 2
            self.part = number % 2
            self.first = ("x", "z")[self.part]
            self.base = 20 * number
            self.started = []

        def rows(self, at, part):
            begin, count = {None: (0, 256), 0: (0, 128), 1: (128, 128)}[part]
            return blocks.at[
                self.stream,
                pl.ds(256 * self.part + begin, count),
                pl.ds(pl.multiple_of(at * INNER, INNER), INNER),
            ]

        def copy(self, index, along, across, part, step_along, step_across):
            ref = self.rows(place(self.first, along, across), part)
            return remote(
                ref, ref, ring_send.at[self.base + index], ring_recv.at[self.base + index],
                neighbour(self.first, step_along, step_across),
            )

        def send(self, *args):
            copy = self.copy(*args)
            copy.start()
            self.started.append(copy)

        def arrived(self, index, along, across, part):
            self.copy(index, along, across, part, 1, 0).wait_recv()

        def send_line(self, which, along):
            self.send(4 + 4 * which, along, 0, None, 0, 1)
            self.send(5 + 4 * which, along, 0, None, 0, -1)

        def pass_line(self, which, along):
            self.arrived(4 + 4 * which, along, -1, None)
            self.send(6 + 4 * which, along, -1, 0, 0, 1)
            self.arrived(5 + 4 * which, along, 1, None)
            self.send(7 + 4 * which, along, 1, 1, 0, -1)

        def end_line(self, which, along):
            self.arrived(6 + 4 * which, along, -2, 0)
            self.arrived(7 + 4 * which, along, 2, 1)

        def begin(self):
            self.send(0, 0, 0, None, 1, 0)
            self.send(1, 0, 0, None, -1, 0)
            self.send_line(0, 0)

        def second(self):
            self.arrived(0, -1, 0, None)
            self.send(2, -1, 0, 0, 1, 0)
            self.send_line(1, -1)
            self.arrived(1, 1, 0, None)
            self.send(3, 1, 0, 1, -1, 0)
            self.send_line(2, 1)
            self.pass_line(0, 0)

        def third(self):
            self.arrived(2, -2, 0, 0)
            self.arrived(3, 2, 0, 1)
            self.send_line(3, 2)
            self.pass_line(1, -1)
            self.pass_line(2, 1)

        def fourth(self):
            self.pass_line(3, 2)

        def end(self):
            self.end_line(0, 0)
            self.end_line(1, -1)
            self.end_line(2, 1)
            self.end_line(3, 2)

    units = [Unit(number) for number in range(4)]

    def weight_copy(stream):
        return remote(
            swap_out.at[stream], swap_in.at[stream], swap_send.at[stream], swap_recv.at[stream],
            device(y_hi, core, z, x, 1 - y_lo),
        )

    def weight_sum(stream, half):
        return jnp.dot(
            blocks[stream], plane[half].reshape(16 * INNER, 256), preferred_element_type=jnp.float32
        )

    def weight_send(stream):
        swap_out[stream] = weight_sum(stream, 1 - y_lo).astype(jnp.bfloat16)
        weight_copy(stream).start()
        sums[stream] = weight_sum(stream, y_lo)

    def weight_end(stream):
        weight_copy(stream).wait_recv()
        full = sums[stream] + swap_in[stream].astype(jnp.float32)
        wgrad_ref[:, stream * 512 : (stream + 1) * 512] = full.T.astype(jnp.bfloat16)

    def product(q, put, first, last):
        held = blocks[:, :, lanes].reshape(1024, INNER)
        for i in range(first, last):
            at = pl.ds(pl.multiple_of(q * part + i * CHUNK, CHUNK), CHUNK)
            put(
                pl.ds(i * CHUNK, CHUNK),
                jnp.dot(wide[at, :], held, preferred_element_type=jnp.float32),
            )

    def to_sibling(which):
        return remote(
            leaving.at[which], arriving.at[which], sib_send.at[which], sib_recv.at[which], sibling
        )

    def for_sibling(which, y, first, last):
        def put(at, value):
            leaving[which, at, :] = value.astype(jnp.bfloat16)

        product(2 * y + 1 - core, put, first, last)
        if last == chunks:
            to_sibling(which).start()

    def keep(y, first, last):
        def put(at, value):
            own[at, :] = value

        product(2 * y + core, put, first, last)

    far_copy = remote(far_out, far_in, far_sem.at[0], far_sem.at[1], opposite)

    units[0].begin()
    units[1].begin()
    for_sibling(0, 1 - y_hi, 0, 4)
    units[0].second()
    units[1].second()
    units[2].begin()
    units[3].begin()
    keep(1 - y_hi, 0, 4)
    units[0].third()
    units[1].third()
    to_sibling(0).wait_recv()
    far_out[...] = (own[...] + arriving[0].astype(jnp.float32)).astype(jnp.bfloat16)
    far_copy.start()
    units[2].second()
    units[3].second()
    units[0].fourth()
    units[1].fourth()
    for_sibling(1, y_hi, 0, 4)
    units[2].third()
    units[3].third()
    units[0].end()
    units[1].end()
    plane_copy.wait_recv()
    weight_send(0)
    units[2].fourth()
    units[3].fourth()
    keep(y_hi, 0, 4)
    to_sibling(1).wait_recv()
    own[...] += arriving[1].astype(jnp.float32)
    units[2].end()
    units[3].end()
    weight_send(1)
    weight_end(0)
    far_copy.wait_recv()
    for i in range(chunks):
        at = pl.ds(i * CHUNK, CHUNK)
        tgrad_ref[:, i * CHUNK : (i + 1) * CHUNK] = (
            (own[at, :] + far_in[at, :].astype(jnp.float32)).T.astype(jnp.bfloat16)
        )

    @pl.loop(1, 32)
    def _(i):
        proj_copy(i).wait_send()
        back_copy(i).wait_send()
        gated_copy(i).wait()

    for copy in pieces + passed + [token_pair, plane_copy, far_copy]:
        copy.wait_send()
    spread_done(0, dp)
    spread_done(1, far)
    for unit in units:
        for copy in unit.started:
            copy.wait_send()
    for i in range(2):
        to_sibling(i).wait_send()
        weight_copy(i).wait_send()
    weight_end(1)


def on_device(tokens, in_weight, short_taps, filters, cotangent):
    channels, length = filters.shape
    groups = lax.axis_size("context")
    rows, part = tokens.shape
    depth, streams, slab = in_weight.shape
    tiles = slab // INNER
    flat = (
        in_weight.reshape(depth, streams, tiles, INNER)
        .transpose(0, 2, 1, 3)
        .reshape(depth * streams * tiles, INNER)
    )
    taps = lax.dynamic_slice_in_dim(short_taps, lax.axis_index("context") * channels, channels, axis=2)
    taps = jnp.broadcast_to(taps[..., None], taps.shape + (INNER,))
    matrices, turns = tables()
    vmem = pl.BlockSpec(memory_space=pltpu.VMEM)
    hbm = pl.BlockSpec(memory_space=pl.ANY)

    def bf16(*shape):
        return pltpu.VMEM(shape, jnp.bfloat16)

    def f32(*shape):
        return pltpu.VMEM(shape, jnp.float32)

    def dma(*counts):
        return [pltpu.SemaphoreType.DMA((count,)) for count in counts]

    size = ROWS * channels
    gated_out, token_grad, weight_grad, filter_grad = pl.pallas_call(
        block_kernel,
        out_shape=(
            jax.ShapeDtypeStruct((groups, channels, rows), jnp.bfloat16),
            jax.ShapeDtypeStruct((rows, part), jnp.bfloat16),
            jax.ShapeDtypeStruct((256, streams * slab), jnp.bfloat16),
            jax.ShapeDtypeStruct((channels, length), jnp.float32),
        ),
        in_specs=[hbm, hbm, vmem, vmem, vmem, vmem, hbm],
        out_specs=[vmem] * 4,
        scratch_shapes=[
            bf16(4, CHUNK * 8, INNER),
            f32(CHUNK * 8, INNER),
            bf16(depth, streams * slab),
            bf16(4, rows, part),
            bf16(streams, groups, channels, rows),
            f32(rows, streams * slab),
            bf16(2, 16, rows, 256),
            bf16(groups, streams, channels, rows),
            bf16(groups, channels, rows),
            f32(3, HALF, channels, INNER),
            f32(3, size, 2 * INNER),
            f32(3, size, 2 * INNER),
            f32(HALF, channels, INNER),
            bf16(groups, 3, channels, rows),
            bf16(streams, slab, 16 * rows),
            f32(streams, slab, 256),
            bf16(2, part, rows),
            bf16(2, part, rows),
            bf16(part, rows),
            bf16(part, rows),
            f32(part, rows),
            bf16(streams, slab, 256),
            bf16(streams, slab, 256),
            *dma(4, 2, 2, PIECES, PIECES, PIECES, PIECES, 16, 16, 2, 32, 32, 32, 32),
            *dma(32, 32, 32, 32, 2, 2, 2, 80, 80, 2, 2),
        ],
        compiler_params=pltpu.CompilerParams(
            collective_id=0, has_side_effects=True, vmem_limit_bytes=56 * 1024 * 1024
        ),
        cost_estimate=pl.CostEstimate(
            flops=8_000_000_000, bytes_accessed=24_000_000, transcendentals=0
        ),
        name="block_forward_backward",
    )(
        tokens, cotangent.reshape(groups, channels, rows), filters, taps,
        jnp.asarray(matrices), jnp.asarray(turns), flat,
    )
    return (
        gated_out.reshape(slab, rows),
        token_grad,
        weight_grad.reshape(weight_grad.shape[0], streams, slab),
        filter_grad,
    )


def solution(mesh):
    placed = (
        P("context", "dp"),
        P(None, None, "dp"),
        P(None, None, "dp"),
        P(("dp", "context"), None),
        P("dp", "context"),
    )
    return jax.shard_map(
        on_device,
        mesh=mesh,
        in_specs=placed,
        out_specs=(
            P("dp", "context"),
            P("context", "dp"),
            P("context", None, "dp"),
            P(("dp", "context"), None),
        ),
        check_vma=False,
    )
```

time: 116 us -> 102 us (0.88)
  Pallas kernels: 110 us -> 92 us
  local copies, waits for them, and re-layouts: 5.42 us -> 8.82 us
    pallas_call x3 -> x1, Pallas kernels: 110 us -> 92 us  [on_device(): pl.pallas_call(block_kernel, out_shape=(jax.ShapeDtypeStruct((groups, cha...]
    unnamed x14 -> x5, local copies, waits for them, and re-layouts: 4.1 us -> 5.82 us
where the time goes in v3:
time: 102 us; the launch traced here: 101 us
  Pallas kernels  92 us (90%)
  local copies, waits for them, and re-layouts  8.82 us (9%)
    pallas_call x1, Pallas kernels, on_device(): pl.pallas_call(block_kernel, out_shape=(jax.ShapeDtypeStruct((groups, cha...  92 us
    unnamed x5, local copies, waits for them, and re-layouts  5.82 us
    reshape x1, local copies, waits for them, and re-layouts, on_device(): weight_grad.reshape(weight_grad.shape[0], streams, slab)  2.22 us

profile of v3, /device:TPU:0, one launch (start us, length us, event | category | flops | bytes accessed | tf_op | source)
XLA Modules:
  0.0 101.5 jit_solution(2078271766352478603)
XLA Ops:
  0.6 0.0 copy-start
  0.6 0.7 copy-done
  1.3 0.1 constant_dynamic-slice_fusion
  1.4 0.7 broadcast_in_dim.2.taps_ref
  2.1 92.0 %block_forward_backward.1 = (bf16[32,16,128]{2,1,0:T(8,128)(2,1)}, bf16[128,2048]{1,0:T(8,128)(2,1)}, bf16[256,1024]{1,0:T(8,128)(2,1)}, f32[16,4096]{1,0:T(8,128)}) custom-call(bf16[128,2048]{1,0:T(8,128)(2,1)} %tok_ref.1, bf16[32,16,128]{2,1,0:T(8,128)(2,1)} %bitcast.9, f32[16,4096]{1,0:T(8,128)} %filt_ref.1, f32[2,3,16,128]{3,2,1,0:T(8,128)} %broadcast_in_dim.2.taps_ref, ...), custom_call_target="tpu_custom_call" | custom-call | flops 8000000000 | bytes 24000000 | tf_op jit(solution)/shard_map/block_forward_backward/pallas_call | solution.py:759
  94.1 2.2 %reshape.28 = bf16[256,2,512]{2,1,0:T(2,128)(2,1)} reshape(bf16[256,1024]{1,0:T(8,128)(2,1)} %get-tuple-element.10) | data formatting | bytes 1048576 | tf_op jit(solution)/shard_map/reshape | solution.py:810
  96.3 1.6 %copy.16 = bf16[512,128]{1,0:T(8,128)(2,1)} copy(bf16[512,128]{1,0:T(8,128)(2,1)} %bitcast.7) | data formatting | bytes 262144
  97.9 1.9 %copy.17 = bf16[128,2048]{1,0:T(8,128)(2,1)} copy(bf16[128,2048]{1,0:T(8,128)(2,1)} %get-tuple-element.17) | data formatting | bytes 1048576
  99.8 1.7 %copy.18 = f32[16,4096]{1,0:T(8,128)} copy(f32[16,4096]{1,0:T(8,128)} %get-tuple-element.19) | data formatting | bytes 524288
  (1 shorter events, 0.0 us)
Async XLA Ops:
  0.6 0.7 copy-start

commit v4 on v3

--- a/solution.py
+++ b/solution.py
@@ -223,11 +223,12 @@
 
 
 def block_kernel(
-    tok_ref, cot_ref, filt_ref, taps_ref, mat_ref, turn_ref, flat_ref,
-    gated_ref, tgrad_ref, wgrad_ref, fgrad_ref,
+    tok_ref, cot_ref, filt_hbm, taps_ref, mat_hbm, turn_hbm, flat_ref,
+    gated_hbm, tgrad_hbm, wgrad_hbm, fgrad_hbm,
+    filt_ref, mat_ref, turn_ref, gated_ref, tgrad_ref, wgrad_ref, wgrad_rows, fgrad_ref, out_sem,
     stage, loose, wide, gathered, outgoing, total, plane, proj, cot,
-    fields, spec, prod, gate_ref, back,
-    blocks, sums, leaving, arriving, far_out, far_in, own, swap_out, swap_in,
+    fields, spec, prod, gate_ref, gated_group,
+    ours, blocks, held, sums, leaving, arriving, far_out, far_in, own, swap_out, swap_in,
     load_sem, in_sem, pair_sem, half_send, half_recv, pass_send, pass_recv,
     spread_send, spread_recv, plane_sem, proj_send, proj_recv, cot_send, cot_recv,
     back_send, back_recv, gated_send, gated_recv, sib_send, sib_recv, far_sem,
@@ -237,11 +238,11 @@
     dp = lax.axis_index("dp")
     context = lax.axis_index("context")
     rows, part = tok_ref.shape
-    channels = filt_ref.shape[0]
+    channels = filt_hbm.shape[0]
+    size = ROWS * channels
     sibling = device(y_hi, 1 - core, z, x, y_lo)
     opposite = device(1 - y_hi, core, z, x, y_lo)
     slot = z * 4 + x
-    lanes = pl.ds(pl.multiple_of(slot * INNER, INNER), INNER)
     chunks = part // CHUNK
     flat_rows = CHUNK * 8
 
@@ -255,7 +256,11 @@
         at = pl.ds(pl.multiple_of(chunk_of(step) * flat_rows, flat_rows), flat_rows)
         return pltpu.make_async_copy(flat_ref.at[at], stage.at[step % 4], load_sem.at[step % 4])
 
-    def separate(first, last):
+    def cot_copy(i):
+        to = lax.rem(context + i, 32)
+        return remote(cot_ref.at[to], cot.at[context], cot_send.at[i], cot_recv.at[i], (dp, to))
+
+    def separate(first, last, sends=False):
         @pl.loop(first, last)
         def _(step):
             load(step).wait()
@@ -272,6 +277,13 @@
             def _():
                 load(step + 4).start()
 
+            for j in range(4 if sends else 0):
+                to = 1 + (step - first) * 4 + j
+
+                @pl.when(to < 32)
+                def _():
+                    cot_copy(to).start()
+
     def multiply(j, first, last):
         for piece in range(first, last):
             at = pl.ds(pl.multiple_of((quarter(j) * chunks + piece) * CHUNK, CHUNK), CHUNK)
@@ -283,10 +295,16 @@
 
     own_tokens = pltpu.make_async_copy(tok_ref, gathered.at[dp], in_sem.at[0])
     own_cot = pltpu.make_async_copy(cot_ref.at[context], cot.at[context], in_sem.at[1])
+    own_tables = [
+        pltpu.make_async_copy(src, dst, in_sem.at[2 + i])
+        for i, (src, dst) in enumerate(((filt_hbm, filt_ref), (mat_hbm, mat_ref), (turn_hbm, turn_ref)))
+    ]
+    for step in range(4):
+        load(step).start()
     own_tokens.start()
     own_cot.start()
-    for step in range(4):
-        load(step).start()
+    for copy in own_tables:
+        copy.start()
     greet_line()
 
     @pl.loop(1, 16)
@@ -294,6 +312,7 @@
         other = lax.rem(slot + i, 16)
         greet(device(y_hi, 1 - core, other // 4, other % 4, y_lo))
 
+    separate(0, 3)
     pl.semaphore_wait(pltpu.get_barrier_semaphore(), 34 + 15)
 
     width = part // PIECES
@@ -355,38 +374,48 @@
             def _():
                 there.wait_send()
 
-    plane_copy = remote(plane.at[core], plane.at[core], plane_sem.at[0], plane_sem.at[1], sibling)
+    across = device(y_hi, core, z, x, 1 - y_lo)
+    plane_pair = remote(plane.at[core], plane.at[core], plane_sem.at[0], plane_sem.at[1], sibling)
 
     spread_start(0, dp, 0, 8)
 
-    def cot_copy(i):
-        to = lax.rem(context + i, 32)
-        return remote(cot_ref.at[to], cot.at[context], cot_send.at[i], cot_recv.at[i], (dp, to))
-
-    @pl.loop(1, 32)
-    def _(i):
-        cot_copy(i).start()
-
     total[...] = jnp.zeros_like(total)
-    separate(0, 4)
+    separate(3, 11, True)
     multiply(0, 0, 4)
-    separate(4, 7)
     token_pair.wait_recv()
-    for n in range(HALF):
-        fields[0, n] = filt_ref[:, n * INNER : (n + 1) * INNER]
     for i in range(PIECES):
-        separate(7 + (9 * i) // PIECES, 7 + (9 * (i + 1)) // PIECES)
-        if i == PIECES - 1:
+        if i < 3:
+            pieces[i].wait_recv()
+            passed[i].start()
+            spread_start(1, far, 2 * i, 2 * i + 2)
+            separate(11 + i, 12 + i)
+        else:
+            separate(14, 16)
             multiply(1, 0, 4)
             multiply(2, 0, 3)
-        pieces[i].wait_recv()
-        passed[i].start()
-        if i % 2 == 1 and PIECES == 4:
-            spread_start(1, far, 2 * i - 2, 2 * i + 2)
-    multiply(2, 3, 4)
-    for i in range(PIECES):
-        passed[i].wait_recv()
-        multiply(3, i, i + 1)
+            for n in range(3):
+                passed[n].wait_recv()
+                multiply(3, n, n + 1)
+            pieces[i].wait_recv()
+            passed[i].start()
+            multiply(2, 3, 4)
+            passed[3].wait_recv()
+            multiply(3, 3, 4)
+    def transform(begin, end):
+        @pl.loop(begin, end)
+        def _(which):
+            for row, (re, im) in enumerate(outer_forward(lambda n: fields[which, n])):
+                cos = turn_ref[0, row][None, :]
+                sin = turn_ref[1, row][None, :]
+                at = pl.ds(row * channels, channels)
+                if im is None:
+                    spec[which, at, :INNER] = re * cos
+                    spec[which, at, INNER:] = -(re * sin)
+                else:
+                    spec[which, at, :INNER] = re * cos + im * sin
+                    spec[which, at, INNER:] = im * cos - re * sin
+            spec[which] = times_matrix(spec[which], mat_ref[0], mat_ref[1])
+
     outgoing[...] = total[...].T.astype(jnp.bfloat16).reshape(outgoing.shape)
 
     def proj_copy(i):
@@ -398,10 +427,15 @@
         proj_copy(i).start()
 
     proj[context] = outgoing[:, context]
+    spread_start(1, far, 6, 8)
+    for copy in own_tables:
+        copy.wait()
+    for n in range(HALF):
+        fields[0, n] = filt_ref[:, n * INNER : (n + 1) * INNER]
 
     @pl.loop(1, 32)
     def _(i):
-        cot_copy(i).wait()
+        cot_copy(i).wait_recv()
 
     own_cot.wait()
 
@@ -423,21 +457,7 @@
         fields[2, n] = cot[n].astype(jnp.float32) * gate
         fields[1, n] = short(1, n)
 
-    size = ROWS * channels
-
-    @pl.loop(0, 3)
-    def _(which):
-        for row, (re, im) in enumerate(outer_forward(lambda n: fields[which, n])):
-            cos = turn_ref[0, row][None, :]
-            sin = turn_ref[1, row][None, :]
-            at = pl.ds(row * channels, channels)
-            if im is None:
-                spec[which, at, :INNER] = re * cos
-                spec[which, at, INNER:] = -(re * sin)
-            else:
-                spec[which, at, :INNER] = re * cos + im * sin
-                spec[which, at, INNER:] = im * cos - re * sin
-        spec[which] = times_matrix(spec[which], mat_ref[0], mat_ref[1])
+    transform(0, 3)
 
     @pl.loop(0, ROWS)
     def _(row):
@@ -470,7 +490,7 @@
 
     for n in range(HALF):
         entry = fields[0, n]
-        back[n, 2] = (gate_ref[n] * entry).astype(back.dtype)
+        gated_group[n] = (gate_ref[n] * entry).astype(jnp.bfloat16)
         gate_ref[n] = cot[n].astype(jnp.float32) * entry
 
     for stream, load_row in enumerate((lambda n: gate_ref[n], lambda n: fields[1, n])):
@@ -480,89 +500,79 @@
             result = taps_ref[stream, 0] * here
             for lead in (1, 2):
                 result = result + taps_ref[stream, lead] * led(here, after, lead)
-            back[n, stream] = result.astype(jnp.bfloat16)
+            column = n // 2 * INNER
+            ours[stream, n % 2, :, column : column + INNER] = result.astype(jnp.bfloat16)
 
     def group_rows(group):
         return pl.ds(pl.multiple_of(group * channels, channels), channels)
 
+    def column_of(index):
+        return pl.ds(pl.multiple_of(index // 2 * INNER, INNER), INNER)
+
     def back_copy(i):
         to = lax.rem(context + i, 32)
-        to_slot = (to // 8) * 4 + (to // 2) % 4
-        to_lanes = pl.ds(pl.multiple_of(to_slot * INNER, INNER), INNER)
         return remote(
-            back.at[to, pl.ds(0, 2)], blocks.at[:, group_rows(context), to_lanes],
+            ours.at[:, to % 2, :, column_of(to)], held.at[:, group_rows(context)],
             back_send.at[i], back_recv.at[i], (dp, to),
         )
 
     def back_arrival(i):
         source = lax.rem(context + 32 - i, 32)
         return remote(
-            back.at[source, pl.ds(0, 2)], blocks.at[:, group_rows(source), lanes],
+            ours.at[:, source % 2, :, column_of(source)], held.at[:, group_rows(source)],
             back_send.at[i], back_recv.at[i], (dp, source),
         )
+
+    ours_across = remote(
+        ours.at[:, 1 - y_lo], blocks.at[:, group_rows(context)], plane_sem.at[2], plane_sem.at[3], across
+    )
 
     def gated_copy(i):
         to = lax.rem(context + i, 32)
         return remote(
-            back.at[to, 2], gated_ref.at[context], gated_send.at[i], gated_recv.at[i], (dp, to)
+            gated_group.at[to], gated_ref.at[context], gated_send.at[i], gated_recv.at[i], (dp, to)
         )
 
+    def leave(which):
+        src, dst = (
+            (gated_ref, gated_hbm), (tgrad_ref, tgrad_hbm), (wgrad_ref, wgrad_hbm), (fgrad_ref, fgrad_hbm),
+        )[which]
+        return pltpu.make_async_copy(src, dst, out_sem.at[which])
+
     @pl.loop(1, 32)
     def _(i):
         back_copy(i).start()
 
-    blocks[:, group_rows(context), lanes] = back[context, pl.ds(0, 2)]
-
-    @pl.loop(1, 32)
-    def _(i):
-        gated_copy(i).start()
-
-    gated_ref[context] = back[context, 2]
-    for n in range(HALF):
-        fgrad_ref[:, n * INNER : (n + 1) * INNER] = fields[2, n]
-
-    @pl.loop(0, 16)
-    def _(i):
-        remote(
-            plane.at[core, i], plane.at[core, i], spread_send.at[0], spread_recv.at[i], sibling
-        ).wait_recv()
-
-    plane_copy.start()
-
-    @pl.loop(1, 32)
-    def _(i):
-        back_arrival(i).wait_recv()
-
-    def place(first, along, across):
+    ours_across.start()
+    blocks[:, group_rows(context)] = ours[:, y_lo]
+
+    def place(first, along, aside):
         if first == "x":
-            return lax.rem(z + across + 4, 4) * 4 + lax.rem(x + along + 4, 4)
-        return lax.rem(z + along + 4, 4) * 4 + lax.rem(x + across + 4, 4)
-
-    def neighbour(first, along, across):
-        at = place(first, along, across)
+            return lax.rem(z + aside + 4, 4) * 4 + lax.rem(x + along + 4, 4)
+        return lax.rem(z + along + 4, 4) * 4 + lax.rem(x + aside + 4, 4)
+
+    def neighbour(first, along, aside):
+        at = place(first, along, aside)
         return device(y_hi, core, at // 4, at % 4, y_lo)
 
     class Unit:
         def __init__(self, number):
             self.stream = number // 2
-            self.part = number % 2
-            self.first = ("x", "z")[self.part]
+            self.from_y = (y_lo, 1 - y_lo)[number % 2]
+            self.first = ("x", "z")[number % 2]
             self.base = 20 * number
             self.started = []
 
-        def rows(self, at, part):
-            begin, count = {None: (0, 256), 0: (0, 128), 1: (128, 128)}[part]
-            return blocks.at[
+        def copy(self, index, along, aside, part, step_along, step_aside):
+            begin, count = {None: (0, 2048), 0: (0, 1024), 1: (1024, 1024)}[part]
+            ref = blocks.at[
                 self.stream,
-                pl.ds(256 * self.part + begin, count),
-                pl.ds(pl.multiple_of(at * INNER, INNER), INNER),
+                group_rows(2 * place(self.first, along, aside) + self.from_y),
+                pl.ds(begin, count),
             ]
-
-        def copy(self, index, along, across, part, step_along, step_across):
-            ref = self.rows(place(self.first, along, across), part)
             return remote(
                 ref, ref, ring_send.at[self.base + index], ring_recv.at[self.base + index],
-                neighbour(self.first, step_along, step_across),
+                neighbour(self.first, step_along, step_aside),
             )
 
         def send(self, *args):
@@ -570,8 +580,8 @@
             copy.start()
             self.started.append(copy)
 
-        def arrived(self, index, along, across, part):
-            self.copy(index, along, across, part, 1, 0).wait_recv()
+        def arrived(self, index, along, aside, part):
+            self.copy(index, along, aside, part, 1, 0).wait_recv()
 
         def send_line(self, which, along):
             self.send(4 + 4 * which, along, 0, None, 0, 1)
@@ -583,46 +593,35 @@
             self.arrived(5 + 4 * which, along, 1, None)
             self.send(7 + 4 * which, along, 1, 1, 0, -1)
 
-        def end_line(self, which, along):
-            self.arrived(6 + 4 * which, along, -2, 0)
-            self.arrived(7 + 4 * which, along, 2, 1)
-
         def begin(self):
             self.send(0, 0, 0, None, 1, 0)
             self.send(1, 0, 0, None, -1, 0)
-            self.send_line(0, 0)
-
-        def second(self):
+
+        def relay(self):
             self.arrived(0, -1, 0, None)
             self.send(2, -1, 0, 0, 1, 0)
-            self.send_line(1, -1)
             self.arrived(1, 1, 0, None)
             self.send(3, 1, 0, 1, -1, 0)
+
+        def lines(self):
+            self.send_line(1, -1)
             self.send_line(2, 1)
-            self.pass_line(0, 0)
-
-        def third(self):
+
+        def last_line(self):
             self.arrived(2, -2, 0, 0)
             self.arrived(3, 2, 0, 1)
             self.send_line(3, 2)
-            self.pass_line(1, -1)
-            self.pass_line(2, 1)
-
-        def fourth(self):
-            self.pass_line(3, 2)
 
         def end(self):
-            self.end_line(0, 0)
-            self.end_line(1, -1)
-            self.end_line(2, 1)
-            self.end_line(3, 2)
+            for which, along in enumerate((0, -1, 1, 2)):
+                self.arrived(6 + 4 * which, along, -2, 0)
+                self.arrived(7 + 4 * which, along, 2, 1)
 
     units = [Unit(number) for number in range(4)]
 
     def weight_copy(stream):
         return remote(
-            swap_out.at[stream], swap_in.at[stream], swap_send.at[stream], swap_recv.at[stream],
-            device(y_hi, core, z, x, 1 - y_lo),
+            swap_out.at[stream], swap_in.at[stream], swap_send.at[stream], swap_recv.at[stream], across
         )
 
     def weight_sum(stream, half):
@@ -637,96 +636,183 @@
 
     def weight_end(stream):
         weight_copy(stream).wait_recv()
-        full = sums[stream] + swap_in[stream].astype(jnp.float32)
-        wgrad_ref[:, stream * 512 : (stream + 1) * 512] = full.T.astype(jnp.bfloat16)
+        turned_sum = (sums[stream] + swap_in[stream].astype(jnp.float32)).T
+        for tile in range(4):
+            wgrad_rows[pl.ds(2 * tile + stream, 256, stride=8), :] = turned_sum[
+                :, tile * INNER : (tile + 1) * INNER
+            ]
 
     def product(q, put, first, last):
-        held = blocks[:, :, lanes].reshape(1024, INNER)
+        shard = held[...].reshape(1024, INNER)
         for i in range(first, last):
             at = pl.ds(pl.multiple_of(q * part + i * CHUNK, CHUNK), CHUNK)
             put(
                 pl.ds(i * CHUNK, CHUNK),
-                jnp.dot(wide[at, :], held, preferred_element_type=jnp.float32),
+                jnp.dot(wide[at, :], shard, preferred_element_type=jnp.float32),
             )
 
-    def to_sibling(which):
+    def chunk_rows(i):
+        return pl.ds(i * CHUNK, CHUNK)
+
+    def to_sibling(which, i):
+        at = chunk_rows(i)
         return remote(
-            leaving.at[which], arriving.at[which], sib_send.at[which], sib_recv.at[which], sibling
+            leaving.at[which, at], arriving.at[which, at],
+            sib_send.at[4 * which + i], sib_recv.at[4 * which + i], sibling,
         )
 
-    def for_sibling(which, y, first, last):
+    def for_sibling(which, y):
         def put(at, value):
             leaving[which, at, :] = value.astype(jnp.bfloat16)
 
-        product(2 * y + 1 - core, put, first, last)
-        if last == chunks:
-            to_sibling(which).start()
-
-    def keep(y, first, last):
+        for i in range(chunks):
+            product(2 * y + 1 - core, put, i, i + 1)
+            to_sibling(which, i).start()
+
+    def keep(which, y, i):
         def put(at, value):
             own[at, :] = value
 
-        product(2 * y + core, put, first, last)
-
-    far_copy = remote(far_out, far_in, far_sem.at[0], far_sem.at[1], opposite)
+        product(2 * y + core, put, i, i + 1)
+        to_sibling(which, i).wait_recv()
+
+    def far_copy(i):
+        at = chunk_rows(i)
+        return remote(far_out.at[at], far_in.at[at], far_sem.at[i], far_sem.at[4 + i], opposite)
 
     units[0].begin()
+    units[2].begin()
+    units[0].send_line(0, 0)
+    held[:, group_rows(context)] = ours[:, y_lo, :, column_of(context)]
+    gated_ref[context] = gated_group[context]
+    for n in range(HALF):
+        fgrad_ref[:, n * INNER : (n + 1) * INNER] = fields[2, n]
+    leave(3).start()
+
+    @pl.loop(0, 16)
+    def _(i):
+        ref = plane.at[core, i]
+        remote(ref, ref, spread_send.at[0], spread_recv.at[i], sibling).wait_recv()
+
+    plane_pair.start()
+    ours_across.wait_recv()
     units[1].begin()
-    for_sibling(0, 1 - y_hi, 0, 4)
-    units[0].second()
-    units[1].second()
-    units[2].begin()
     units[3].begin()
-    keep(1 - y_hi, 0, 4)
-    units[0].third()
-    units[1].third()
-    to_sibling(0).wait_recv()
-    far_out[...] = (own[...] + arriving[0].astype(jnp.float32)).astype(jnp.bfloat16)
-    far_copy.start()
-    units[2].second()
-    units[3].second()
-    units[0].fourth()
-    units[1].fourth()
-    for_sibling(1, y_hi, 0, 4)
-    units[2].third()
-    units[3].third()
-    units[0].end()
-    units[1].end()
-    plane_copy.wait_recv()
+    for unit in units[1:]:
+        unit.send_line(0, 0)
+    for unit in units[:2]:
+        unit.relay()
+        unit.lines()
+    for unit in units[2:]:
+        unit.relay()
+
+    @pl.loop(1, 32)
+    def _(i):
+        back_arrival(i).wait_recv()
+
+    for_sibling(0, 1 - y_hi)
+    for unit in units[:2]:
+        unit.pass_line(0, 0)
+        unit.last_line()
+    for i in range(chunks):
+        keep(0, 1 - y_hi, i)
+        at = chunk_rows(i)
+        far_out[at, :] = (own[at, :] + arriving[0, at, :].astype(jnp.float32)).astype(jnp.bfloat16)
+        far_copy(i).start()
+    for unit in units[2:]:
+        unit.lines()
+    for unit in units[:2]:
+        unit.pass_line(1, -1)
+        unit.pass_line(2, 1)
+    for unit in units[2:]:
+        unit.pass_line(0, 0)
+        unit.last_line()
+    for unit in units[:2]:
+        unit.pass_line(3, 2)
+
+    @pl.loop(1, 32)
+    def _(i):
+        gated_copy(i).start()
+
+    for unit in units[2:]:
+        unit.pass_line(1, -1)
+        unit.pass_line(2, 1)
+    for_sibling(1, y_hi)
+    for unit in units[2:]:
+        unit.pass_line(3, 2)
+    plane_pair.wait_recv()
+    for unit in units[:2]:
+        unit.end()
     weight_send(0)
-    units[2].fourth()
-    units[3].fourth()
-    keep(y_hi, 0, 4)
-    to_sibling(1).wait_recv()
-    own[...] += arriving[1].astype(jnp.float32)
-    units[2].end()
-    units[3].end()
+    for i in range(chunks):
+        keep(1, y_hi, i)
+        at = chunk_rows(i)
+        own[at, :] += arriving[1, at, :].astype(jnp.float32)
+
+    @pl.loop(1, 32)
+    def _(i):
+        cot_copy(i).wait_send()
+        proj_copy(i).wait_send()
+        back_copy(i).wait_send()
+        gated_copy(i).wait()
+
+    leave(0).start()
+    for copy in pieces + passed + [token_pair, plane_pair, ours_across]:
+        copy.wait_send()
+    spread_done(0, dp)
+    spread_done(1, far)
+    for unit in units[2:]:
+        unit.end()
     weight_send(1)
     weight_end(0)
-    far_copy.wait_recv()
     for i in range(chunks):
-        at = pl.ds(i * CHUNK, CHUNK)
+        far_copy(i).wait_recv()
+        at = chunk_rows(i)
         tgrad_ref[:, i * CHUNK : (i + 1) * CHUNK] = (
             (own[at, :] + far_in[at, :].astype(jnp.float32)).T.astype(jnp.bfloat16)
         )
-
-    @pl.loop(1, 32)
-    def _(i):
-        proj_copy(i).wait_send()
-        back_copy(i).wait_send()
-        gated_copy(i).wait()
-
-    for copy in pieces + passed + [token_pair, plane_copy, far_copy]:
-        copy.wait_send()
-    spread_done(0, dp)
-    spread_done(1, far)
+    leave(1).start()
     for unit in units:
         for copy in unit.started:
             copy.wait_send()
+    for i in range(chunks):
+        far_copy(i).wait_send()
+        for which in range(2):
+            to_sibling(which, i).wait_send()
     for i in range(2):
-        to_sibling(i).wait_send()
         weight_copy(i).wait_send()
     weight_end(1)
+    wgrad_ref[...] = wgrad_rows[...].astype(jnp.bfloat16)
+    leave(2).start()
+    for i in range(4):
+        leave(i).wait()
+
+
+def finish_kernel(*refs):
+    sources, targets, held, sem = refs[:4], refs[4:8], refs[8:12], refs[12]
+    arrive = [pltpu.make_async_copy(a, b, sem.at[i]) for i, (a, b) in enumerate(zip(sources, held))]
+    depart = [pltpu.make_async_copy(a, b, sem.at[4 + i]) for i, (a, b) in enumerate(zip(held, targets))]
+    for copy in arrive:
+        copy.start()
+    for first, second in zip(arrive, depart):
+        first.wait()
+        second.start()
+    for copy in depart:
+        copy.wait()
+
+
+def finished(*arrays):
+    hbm = pl.BlockSpec(memory_space=pl.ANY)
+    return pl.pallas_call(
+        finish_kernel,
+        out_shape=tuple(jax.ShapeDtypeStruct(array.shape, array.dtype) for array in arrays),
+        in_specs=[hbm] * 4,
+        out_specs=[hbm] * 4,
+        scratch_shapes=[pltpu.VMEM(array.shape, array.dtype) for array in arrays]
+        + [pltpu.SemaphoreType.DMA((8,))],
+        compiler_params=pltpu.CompilerParams(vmem_limit_bytes=56 * 1024 * 1024),
+        name="results",
+    )(*arrays)
 
 
 def on_device(tokens, in_weight, short_taps, filters, cotangent):
@@ -756,17 +842,26 @@
         return [pltpu.SemaphoreType.DMA((count,)) for count in counts]
 
     size = ROWS * channels
-    gated_out, token_grad, weight_grad, filter_grad = pl.pallas_call(
+    results = pl.pallas_call(
         block_kernel,
         out_shape=(
             jax.ShapeDtypeStruct((groups, channels, rows), jnp.bfloat16),
             jax.ShapeDtypeStruct((rows, part), jnp.bfloat16),
-            jax.ShapeDtypeStruct((256, streams * slab), jnp.bfloat16),
+            jax.ShapeDtypeStruct((256 * streams * tiles, INNER), jnp.bfloat16),
             jax.ShapeDtypeStruct((channels, length), jnp.float32),
         ),
-        in_specs=[hbm, hbm, vmem, vmem, vmem, vmem, hbm],
-        out_specs=[vmem] * 4,
+        in_specs=[hbm, hbm, hbm, vmem, hbm, hbm, hbm],
+        out_specs=[hbm] * 4,
         scratch_shapes=[
+            f32(channels, length),
+            bf16(*matrices.shape),
+            f32(*turns.shape),
+            bf16(groups, channels, rows),
+            bf16(rows, part),
+            bf16(256 * streams * tiles, INNER),
+            f32(256 * streams * tiles, INNER),
+            f32(channels, length),
+            *dma(4),
             bf16(4, CHUNK * 8, INNER),
             f32(CHUNK * 8, INNER),
             bf16(depth, streams * slab),
@@ -780,8 +875,10 @@
             f32(3, size, 2 * INNER),
             f32(3, size, 2 * INNER),
             f32(HALF, channels, INNER),
-            bf16(groups, 3, channels, rows),
-            bf16(streams, slab, 16 * rows),
+            bf16(groups, channels, rows),
+            bf16(streams, 2, channels, length // 2),
+            bf16(streams, slab, length // 2),
+            bf16(streams, slab, rows),
             f32(streams, slab, 256),
             bf16(2, part, rows),
             bf16(2, part, rows),
@@ -790,8 +887,8 @@
             f32(part, rows),
             bf16(streams, slab, 256),
             bf16(streams, slab, 256),
-            *dma(4, 2, 2, PIECES, PIECES, PIECES, PIECES, 16, 16, 2, 32, 32, 32, 32),
-            *dma(32, 32, 32, 32, 2, 2, 2, 80, 80, 2, 2),
+            *dma(4, 5, 2, PIECES, PIECES, PIECES, PIECES, 16, 16, 4, 32, 32, 32, 32),
+            *dma(32, 32, 32, 32, 8, 8, 8, 80, 80, 2, 2),
         ],
         compiler_params=pltpu.CompilerParams(
             collective_id=0, has_side_effects=True, vmem_limit_bytes=56 * 1024 * 1024
@@ -804,10 +901,12 @@
         tokens, cotangent.reshape(groups, channels, rows), filters, taps,
         jnp.asarray(matrices), jnp.asarray(turns), flat,
     )
+    gated_out, token_grad, weight_grad, filter_grad = finished(*results)
+    weight_grad = weight_grad.reshape(256, tiles, streams, INNER).transpose(0, 2, 1, 3)
     return (
         gated_out.reshape(slab, rows),
         token_grad,
-        weight_grad.reshape(weight_grad.shape[0], streams, slab),
+        weight_grad.reshape(256, streams, slab),
         filter_grad,
     )
 

time: 102 us -> 94.1 us (0.923)
  local copies, waits for them, and re-layouts: 8.82 us -> 1.48 us
  Pallas kernels: 92 us -> 90.8 us
    unnamed x5 -> x2, local copies, waits for them, and re-layouts: 5.82 us -> 0.7 us
    pallas_call x1, Pallas kernels: 92 us -> 88.6 us  [on_device(): pl.pallas_call(block_kernel, out_shape=(jax.ShapeDtypeStruct((groups, cha...]
    pallas_call x0 -> x1, Pallas kernels: none -> 2.23 us  [finished(): pl.pallas_call(finish_kernel, out_shape=tuple((jax.ShapeDtypeStruct(array...]
    reshape x1 -> x0, local copies, waits for them, and re-layouts: 2.22 us -> none  [on_device(): weight_grad.reshape(weight_grad.shape[0], streams, slab)]
where the time goes in v4:
time: 94.1 us; the launch traced here: 93.1 us
  Pallas kernels  90.8 us (96%)
  local copies, waits for them, and re-layouts  1.48 us (2%)
    pallas_call x1, Pallas kernels, on_device(): pl.pallas_call(block_kernel, out_shape=(jax.ShapeDtypeStruct((groups, cha...  88.6 us
    pallas_call x1, Pallas kernels, finished(): pl.pallas_call(finish_kernel, out_shape=tuple((jax.ShapeDtypeStruct(array...  2.23 us

profile of v4, /device:TPU:0, one launch (start us, length us, event | category | flops | bytes accessed | tf_op | source)
XLA Modules:
  0.0 93.1 jit_solution(3406608027111750129)
XLA Ops:
  0.6 0.0 copy-start
  0.6 0.7 copy-done
  1.3 0.1 constant_dynamic-slice_fusion
  1.4 0.7 broadcast_in_dim.2.taps_ref
  2.1 88.6 %block_forward_backward.1 = (bf16[32,16,128]{2,1,0:T(8,128)(2,1)}, bf16[128,2048]{1,0:T(8,128)(2,1)}, bf16[2048,128]{1,0:T(8,128)(2,1)}, f32[16,4096]{1,0:T(8,128)}) custom-call(bf16[128,2048]{1,0:T(8,128)(2,1)} %tok_ref.1, bf16[32,16,128]{2,1,0:T(8,128)(2,1)} %bitcast.14, f32[16,4096]{1,0:T(8,128)} %filt_hbm.1, f32[2,3,16,128]{3,2,1,0:T(8,128)} %broadcast_in_dim.2.taps_ref, ...), custom_call_target="tpu_custom_call" | custom-call | flops 8000000000 | bytes 24000000 | tf_op jit(solution)/shard_map/block_forward_backward/pallas_call | solution.py:845
  90.7 2.2 %results.1 = (bf16[32,16,128]{2,1,0:T(8,128)(2,1)}, bf16[128,2048]{1,0:T(8,128)(2,1)}, bf16[2048,128]{1,0:T(8,128)(2,1)}, f32[16,4096]{1,0:T(8,128)}) custom-call(bf16[32,16,128]{2,1,0:T(8,128)(2,1)} %get-tuple-element.12.refs_0_, bf16[128,2048]{1,0:T(8,128)(2,1)} %get-tuple-element.13.refs_1_, bf16[2048,128]{1,0:T(8,128)(2,1)} %get-tuple-element.14.refs_2_, ...), custom_call_target="tpu_custom_call" | custom-call | tf_op jit(solution)/shard_map/results/pallas_call | solution.py:806
  (1 shorter events, 0.0 us)
Async XLA Ops:
  0.6 0.7 copy-start

commit v5 on v4

--- a/solution.py
+++ b/solution.py
@@ -223,12 +223,12 @@
 
 
 def block_kernel(
-    tok_ref, cot_ref, filt_hbm, taps_ref, mat_hbm, turn_hbm, flat_ref,
+    tok_ref, cot_ref, filt_hbm, taps_hbm, mat_hbm, turn_hbm, flat_ref,
     gated_hbm, tgrad_hbm, wgrad_hbm, fgrad_hbm,
-    filt_ref, mat_ref, turn_ref, gated_ref, tgrad_ref, wgrad_ref, wgrad_rows, fgrad_ref, out_sem,
+    filt_ref, mat_ref, turn_ref, taps_all, taps_ref, gated_ref, tgrad_ref, wgrad_ref, wgrad_rows, fgrad_ref, out_sem,
     stage, loose, wide, gathered, outgoing, total, plane, proj, cot,
     fields, spec, prod, gate_ref, gated_group,
-    ours, blocks, held, sums, leaving, arriving, far_out, far_in, own, swap_out, swap_in,
+    ours, blocks, held, mixed, sums, leaving, arriving, far_out, far_in, own, swap_out, swap_in,
     load_sem, in_sem, pair_sem, half_send, half_recv, pass_send, pass_recv,
     spread_send, spread_recv, plane_sem, proj_send, proj_recv, cot_send, cot_recv,
     back_send, back_recv, gated_send, gated_recv, sib_send, sib_recv, far_sem,
@@ -297,7 +297,7 @@
     own_cot = pltpu.make_async_copy(cot_ref.at[context], cot.at[context], in_sem.at[1])
     own_tables = [
         pltpu.make_async_copy(src, dst, in_sem.at[2 + i])
-        for i, (src, dst) in enumerate(((filt_hbm, filt_ref), (mat_hbm, mat_ref), (turn_hbm, turn_ref)))
+        for i, (src, dst) in enumerate(((filt_hbm, filt_ref), (mat_hbm, mat_ref), (turn_hbm, turn_ref), (taps_hbm, taps_all)))
     ]
     for step in range(4):
         load(step).start()
@@ -430,6 +430,15 @@
     spread_start(1, far, 6, 8)
     for copy in own_tables:
         copy.wait()
+
+    tile = pl.ds(pl.multiple_of(context // 8 * INNER, INNER), INNER)
+    lane = lax.broadcasted_iota(jnp.int32, (channels, INNER), 1)
+    picked = lane == context % 8 * channels + lax.broadcasted_iota(jnp.int32, (channels, INNER), 0)
+    for stream in range(2):
+        for lag in range(3):
+            line = taps_all[lag, pl.ds(stream, 1), tile]
+            column = jnp.sum(jnp.where(picked, line, 0.0), axis=1, keepdims=True)
+            taps_ref[stream, lag] = jnp.broadcast_to(column, (channels, INNER))
     for n in range(HALF):
         fields[0, n] = filt_ref[:, n * INNER : (n + 1) * INNER]
 
@@ -524,7 +533,7 @@
         )
 
     ours_across = remote(
-        ours.at[:, 1 - y_lo], blocks.at[:, group_rows(context)], plane_sem.at[2], plane_sem.at[3], across
+        ours.at[:, 1 - y_lo], blocks.at[:, slot, y_lo], plane_sem.at[2], plane_sem.at[3], across
     )
 
     def gated_copy(i):
@@ -544,7 +553,7 @@
         back_copy(i).start()
 
     ours_across.start()
-    blocks[:, group_rows(context)] = ours[:, y_lo]
+    blocks[:, slot, y_lo] = ours[:, y_lo]
 
     def place(first, along, aside):
         if first == "x":
@@ -567,7 +576,9 @@
             begin, count = {None: (0, 2048), 0: (0, 1024), 1: (1024, 1024)}[part]
             ref = blocks.at[
                 self.stream,
-                group_rows(2 * place(self.first, along, aside) + self.from_y),
+                place(self.first, along, aside),
+                self.from_y,
+                :,
                 pl.ds(begin, count),
             ]
             return remote(
@@ -619,24 +630,31 @@
 
     units = [Unit(number) for number in range(4)]
 
-    def weight_copy(stream):
+    def weight_copy(which):
         return remote(
-            swap_out.at[stream], swap_in.at[stream], swap_send.at[stream], swap_recv.at[stream], across
+            swap_out.at[which], swap_in.at[which], swap_send.at[which], swap_recv.at[which], across
         )
 
-    def weight_sum(stream, half):
+    def weight_sum(which, half):
         return jnp.dot(
-            blocks[stream], plane[half].reshape(16 * INNER, 256), preferred_element_type=jnp.float32
+            blocks[which // 2, :, (y_lo, 1 - y_lo)[which % 2]].reshape(256, 16 * INNER),
+            plane[half].reshape(16 * INNER, 256),
+            preferred_element_type=jnp.float32,
         )
 
-    def weight_send(stream):
-        swap_out[stream] = weight_sum(stream, 1 - y_lo).astype(jnp.bfloat16)
-        weight_copy(stream).start()
-        sums[stream] = weight_sum(stream, y_lo)
+    def weight_send(which):
+        swap_out[which] = weight_sum(which, 1 - y_lo).astype(jnp.bfloat16)
+        weight_copy(which).start()
+
+    def weight_own(which):
+        sums[which] = weight_sum(which, y_lo)
 
     def weight_end(stream):
-        weight_copy(stream).wait_recv()
-        turned_sum = (sums[stream] + swap_in[stream].astype(jnp.float32)).T
+        for mine, theirs in ((2 * stream + 1, 2 * stream), (2 * stream, 2 * stream + 1)):
+            weight_copy(theirs).wait_recv()
+            value = sums[mine] + swap_in[theirs].astype(jnp.float32)
+            mixed[:, (y_lo, 1 - y_lo)[mine % 2]] = value.reshape(16, channels, 256)
+        turned_sum = mixed[...].reshape(512, 256).T
         for tile in range(4):
             wgrad_rows[pl.ds(2 * tile + stream, 256, stride=8), :] = turned_sum[
                 :, tile * INNER : (tile + 1) * INNER
@@ -741,9 +759,9 @@
     for unit in units[2:]:
         unit.pass_line(3, 2)
     plane_pair.wait_recv()
-    for unit in units[:2]:
-        unit.end()
-    weight_send(0)
+    for i in range(2):
+        units[i].end()
+        weight_send(i)
     for i in range(chunks):
         keep(1, y_hi, i)
         at = chunk_rows(i)
@@ -761,9 +779,13 @@
         copy.wait_send()
     spread_done(0, dp)
     spread_done(1, far)
-    for unit in units[2:]:
-        unit.end()
-    weight_send(1)
+    weight_own(0)
+    weight_own(1)
+    for i in range(2, 4):
+        units[i].end()
+        weight_send(i)
+    weight_own(2)
+    weight_own(3)
     weight_end(0)
     for i in range(chunks):
         far_copy(i).wait_recv()
@@ -779,7 +801,7 @@
         far_copy(i).wait_send()
         for which in range(2):
             to_sibling(which, i).wait_send()
-    for i in range(2):
+    for i in range(4):
         weight_copy(i).wait_send()
     weight_end(1)
     wgrad_ref[...] = wgrad_rows[...].astype(jnp.bfloat16)
@@ -826,10 +848,7 @@
         .transpose(0, 2, 1, 3)
         .reshape(depth * streams * tiles, INNER)
     )
-    taps = lax.dynamic_slice_in_dim(short_taps, lax.axis_index("context") * channels, channels, axis=2)
-    taps = jnp.broadcast_to(taps[..., None], taps.shape + (INNER,))
     matrices, turns = tables()
-    vmem = pl.BlockSpec(memory_space=pltpu.VMEM)
     hbm = pl.BlockSpec(memory_space=pl.ANY)
 
     def bf16(*shape):
@@ -850,12 +869,14 @@
             jax.ShapeDtypeStruct((256 * streams * tiles, INNER), jnp.bfloat16),
             jax.ShapeDtypeStruct((channels, length), jnp.float32),
         ),
-        in_specs=[hbm, hbm, hbm, vmem, hbm, hbm, hbm],
+        in_specs=[hbm] * 7,
         out_specs=[hbm] * 4,
         scratch_shapes=[
             f32(channels, length),
             bf16(*matrices.shape),
             f32(*turns.shape),
+            f32(3, streams, slab),
+            f32(streams, 3, channels, INNER),
             bf16(groups, channels, rows),
             bf16(rows, part),
             bf16(256 * streams * tiles, INNER),
@@ -877,18 +898,19 @@
             f32(HALF, channels, INNER),
             bf16(groups, channels, rows),
             bf16(streams, 2, channels, length // 2),
-            bf16(streams, slab, length // 2),
+            bf16(streams, 16, 2, channels, length // 2),
             bf16(streams, slab, rows),
-            f32(streams, slab, 256),
+            f32(16, 2, channels, 256),
+            f32(4, slab // 2, 256),
             bf16(2, part, rows),
             bf16(2, part, rows),
             bf16(part, rows),
             bf16(part, rows),
             f32(part, rows),
-            bf16(streams, slab, 256),
-            bf16(streams, slab, 256),
-            *dma(4, 5, 2, PIECES, PIECES, PIECES, PIECES, 16, 16, 4, 32, 32, 32, 32),
-            *dma(32, 32, 32, 32, 8, 8, 8, 80, 80, 2, 2),
+            bf16(4, slab // 2, 256),
+            bf16(4, slab // 2, 256),
+            *dma(4, 6, 2, PIECES, PIECES, PIECES, PIECES, 16, 16, 4, 32, 32, 32, 32),
+            *dma(32, 32, 32, 32, 8, 8, 8, 80, 80, 4, 4),
         ],
         compiler_params=pltpu.CompilerParams(
             collective_id=0, has_side_effects=True, vmem_limit_bytes=56 * 1024 * 1024
@@ -898,7 +920,7 @@
         ),
         name="block_forward_backward",
     )(
-        tokens, cotangent.reshape(groups, channels, rows), filters, taps,
+        tokens, cotangent.reshape(groups, channels, rows), filters, short_taps.transpose(1, 0, 2),
         jnp.asarray(matrices), jnp.asarray(turns), flat,
     )
     gated_out, token_grad, weight_grad, filter_grad = finished(*results)

time: 94.1 us -> 90.4 us (0.961)
  Pallas kernels: 90.8 us -> 89 us
  local copies, waits for them, and re-layouts: 1.48 us -> 0 us
    pallas_call x1, Pallas kernels: 88.6 us -> 86.7 us  [on_device(): pl.pallas_call(block_kernel, out_shape=(jax.ShapeDtypeStruct((groups, cha...]
where the time goes in v5:
time: 90.4 us; the launch traced here: 89.8 us
  Pallas kernels  89 us (98%)
    pallas_call x1, Pallas kernels, on_device(): pl.pallas_call(block_kernel, out_shape=(jax.ShapeDtypeStruct((groups, cha...  86.7 us
    pallas_call x1, Pallas kernels, finished(): pl.pallas_call(finish_kernel, out_shape=tuple((jax.ShapeDtypeStruct(array...  2.23 us

profile of v5, /device:TPU:0, one launch (start us, length us, event | category | flops | bytes accessed | tf_op | source)
XLA Modules:
  0.0 89.8 jit_solution(8706101228263758676)
XLA Ops:
  0.6 86.7 %block_forward_backward.1 = (bf16[32,16,128]{2,1,0:T(8,128)(2,1)}, bf16[128,2048]{1,0:T(8,128)(2,1)}, bf16[2048,128]{1,0:T(8,128)(2,1)}, f32[16,4096]{1,0:T(8,128)}) custom-call(bf16[128,2048]{1,0:T(8,128)(2,1)} %tok_ref.1, bf16[32,16,128]{2,1,0:T(8,128)(2,1)} %bitcast.15, f32[16,4096]{1,0:T(8,128)} %filt_hbm.1, f32[3,2,512]{2,1,0:T(2,128)} %bitcast.17, ...), custom_call_target="tpu_custom_call" | custom-call | flops 8000000000 | bytes 24000000 | tf_op jit(solution)/shard_map/block_forward_backward/pallas_call | solution.py:864
  87.4 2.2 %results.1 = (bf16[32,16,128]{2,1,0:T(8,128)(2,1)}, bf16[128,2048]{1,0:T(8,128)(2,1)}, bf16[2048,128]{1,0:T(8,128)(2,1)}, f32[16,4096]{1,0:T(8,128)}) custom-call(bf16[32,16,128]{2,1,0:T(8,128)(2,1)} %get-tuple-element.12.refs_0_, bf16[128,2048]{1,0:T(8,128)(2,1)} %get-tuple-element.13.refs_1_, bf16[2048,128]{1,0:T(8,128)(2,1)} %get-tuple-element.14.refs_2_, ...), custom_call_target="tpu_custom_call" | custom-call | tf_op jit(solution)/shard_map/results/pallas_call | solution.py:828

commit v6 on v5

--- a/solution.py
+++ b/solution.py
@@ -312,7 +312,6 @@
         other = lax.rem(slot + i, 16)
         greet(device(y_hi, 1 - core, other // 4, other % 4, y_lo))
 
-    separate(0, 3)
     pl.semaphore_wait(pltpu.get_barrier_semaphore(), 34 + 15)
 
     width = part // PIECES
@@ -380,6 +379,7 @@
     spread_start(0, dp, 0, 8)
 
     total[...] = jnp.zeros_like(total)
+    separate(0, 3)
     separate(3, 11, True)
     multiply(0, 0, 4)
     token_pair.wait_recv()
@@ -759,7 +759,7 @@
     for unit in units[2:]:
         unit.pass_line(3, 2)
     plane_pair.wait_recv()
-    for i in range(2):
+    for i in range(4):
         units[i].end()
         weight_send(i)
     for i in range(chunks):
@@ -779,13 +779,8 @@
         copy.wait_send()
     spread_done(0, dp)
     spread_done(1, far)
-    weight_own(0)
-    weight_own(1)
-    for i in range(2, 4):
-        units[i].end()
-        weight_send(i)
-    weight_own(2)
-    weight_own(3)
+    for i in range(4):
+        weight_own(i)
     weight_end(0)
     for i in range(chunks):
         far_copy(i).wait_recv()

time: 90.4 us -> 90.5 us (level)
  no operation moved by 1% of the time
where the time goes in v6:
time: 90.5 us; the launch traced here: 89.9 us
  Pallas kernels  89.1 us (98%)
    pallas_call x1, Pallas kernels, on_device(): pl.pallas_call(block_kernel, out_shape=(jax.ShapeDtypeStruct((groups, cha...  86.8 us
    pallas_call x1, Pallas kernels, finished(): pl.pallas_call(finish_kernel, out_shape=tuple((jax.ShapeDtypeStruct(array...  2.23 us

profile of v6, /device:TPU:0, one launch (start us, length us, event | category | flops | bytes accessed | tf_op | source)
XLA Modules:
  0.0 89.9 jit_solution(7208792731873766763)
XLA Ops:
  0.6 86.8 %block_forward_backward.1 = (bf16[32,16,128]{2,1,0:T(8,128)(2,1)}, bf16[128,2048]{1,0:T(8,128)(2,1)}, bf16[2048,128]{1,0:T(8,128)(2,1)}, f32[16,4096]{1,0:T(8,128)}) custom-call(bf16[128,2048]{1,0:T(8,128)(2,1)} %tok_ref.1, bf16[32,16,128]{2,1,0:T(8,128)(2,1)} %bitcast.15, f32[16,4096]{1,0:T(8,128)} %filt_hbm.1, f32[3,2,512]{2,1,0:T(2,128)} %bitcast.17, ...), custom_call_target="tpu_custom_call" | custom-call | flops 8000000000 | bytes 24000000 | tf_op jit(solution)/shard_map/block_forward_backward/pallas_call | solution.py:859
  87.5 2.2 %results.1 = (bf16[32,16,128]{2,1,0:T(8,128)(2,1)}, bf16[128,2048]{1,0:T(8,128)(2,1)}, bf16[2048,128]{1,0:T(8,128)(2,1)}, f32[16,4096]{1,0:T(8,128)}) custom-call(bf16[32,16,128]{2,1,0:T(8,128)(2,1)} %get-tuple-element.12.refs_0_, bf16[128,2048]{1,0:T(8,128)(2,1)} %get-tuple-element.13.refs_1_, bf16[2048,128]{1,0:T(8,128)(2,1)} %get-tuple-element.14.refs_2_, ...), custom_call_target="tpu_custom_call" | custom-call | tf_op jit(solution)/shard_map/results/pallas_call | solution.py:823
